TPU v7x, 256 devices: a whole 4x4x8 slice. The times are simulated.
256 devices in a mesh: gx: 8 (over x, core), gyz: 8 (over y, z_lo), band: 4 (over z_hi).
Axes of the slice: x: 4, y: 4, z: 8 (z_hi: 4, z_lo: 2; z = z_hi * 2 + z_lo), core: 2. Of those that a mesh axis runs over, the one named last changes fastest.
Arguments:
- orbitals: float32 [256, 32, 64, 128], P('band', 'gx', 'gyz'), may hold values from -6 to 6
- v_local: float32 [32, 64, 128], P('gx', 'gyz'), may hold values from 0 to 2
- features: bfloat16 [11, 32, 64, 128], P(None, 'gx', 'gyz'), may hold values from -6 to 6
- w_first: bfloat16 [256, 11], replicated, may hold values from -1.75 to 1.75
- w_hidden: bfloat16 [1, 256, 256], replicated, may hold values from -0.375 to 0.375
- w_last: bfloat16 [256], replicated, may hold values from -0.375 to 0.375
- rotation: float32 [256, 256], replicated, may hold values from -0.375 to 0.375
- assignment: int32 [256], replicated, may hold values from 0 to 255, each once
- degrees: int32 [256], P('band'), may hold values from 4 to 8, as said below
Outputs:
- gram: float32 [256, 256], P('band')
- rotated: float32 [256, 32, 64, 128], P('band', 'gx', 'gyz')
Inputs may be any that keep to these rules, and one draw needn't show every extreme that they name: `degrees`: a filter degree of each slot; some slot has 8 and some has 4. `assignment`: each orbital is held in exactly one slot.
All inputs are finite; a program needn't handle non-finite values.
Results may differ from a plain program's by a relative error of at most 0.0043.
Values may be sent and summed in bfloat16 or wider, within the bound.
No kernel may reach another device: no remote copies, remote signals or barrier semaphores. Data moves between devices by JAX's collectives and lax.ppermute only.
A program may use at most 64 MiB of HBM per device.

v0:
```python
import jax
import jax.numpy as jnp
from jax import lax
from jax.sharding import PartitionSpec as P

DEG = 8


LOWER_EDGE = 2.0
CUT_EDGE = 3.0
UPPER_EDGE = 9.5


def with_halo(block, sides, width):
    for axis, dim in sides:
        count = lax.axis_size(axis)
        forward = [(i, i + 1) for i in range(count - 1)]
        backward = [(target, source) for source, target in forward]
        low = lax.ppermute(
            lax.slice_in_dim(block, block.shape[dim] - width, None, axis=dim), axis, forward
        )
        high = lax.ppermute(lax.slice_in_dim(block, 0, width, axis=dim), axis, backward)
        block = jnp.concatenate([low, block, high], axis=dim)
    return block


def coefficients(count):
    half_width = (UPPER_EDGE - CUT_EDGE) / 2.0
    centre = (UPPER_EDGE + CUT_EDGE) / 2.0
    first = half_width / (LOWER_EDGE - centre)
    factors = [(first / half_width, 0.0)]
    sigma = first
    for rounds in range(1, count):
        updated = 1.0 / (2.0 / first - sigma)
        factors.append((2.0 * updated / half_width, sigma * updated))
        sigma = updated
    return (factors, centre)


def hamiltonian(field, potential):
    padded = with_halo(field, (("gx", 1), ("gyz", 2)), 1)
    padded = jnp.pad(padded, ((0, 0), (0, 0), (0, 0), (1, 1)))
    beside_all = padded[:, 2:, 1:-1, 1:-1] + padded[:, :-2, 1:-1, 1:-1]
    beside_all = beside_all + padded[:, 1:-1, 2:, 1:-1] + padded[:, 1:-1, :-2, 1:-1]
    beside_all = beside_all + padded[:, 1:-1, 1:-1, 2:] + padded[:, 1:-1, 1:-1, :-2]
    return 0.5 * (6.0 * field - beside_all) + potential * field


def network(cell_features, w_first, w_hidden, w_last):
    feature_count = cell_features.shape[0]
    flattened = cell_features.reshape(feature_count, -1)
    hidden = jax.nn.silu(jnp.dot(w_first, flattened, preferred_element_type=jnp.float32)).astype(
        jnp.bfloat16
    )
    hidden = jax.nn.silu(jnp.dot(w_hidden[0], hidden, preferred_element_type=jnp.float32)).astype(
        jnp.bfloat16
    )
    values = jnp.tanh(jnp.dot(w_last[None, :], hidden, preferred_element_type=jnp.float32)[0])
    return values.reshape(cell_features.shape[1:])


def on_device(
    orbitals, v_local, features, w_first, w_hidden, w_last, rotation, assignment, degrees
):
    group = lax.axis_index("band")
    local_slots, size_x, size_y, size_z = orbitals.shape
    total_slots = rotation.shape[0]
    cells = size_x * size_y * size_z
    total_cells = float(cells * lax.axis_size("gx") * lax.axis_size("gyz"))
    xc_field = network(features, w_first, w_hidden, w_last)
    potential = v_local + xc_field
    factors, centre = coefficients(DEG)
    previous = orbitals
    current = orbitals
    for rounds in range(DEG):
        image = hamiltonian(current, potential)
        scale_new, scale_old = factors[rounds]
        updated = scale_new * (image - centre * current) - scale_old * previous
        active = (degrees > rounds)[:, None, None, None]
        previous = jnp.where(active, current, previous)
        current = jnp.where(active, updated, current)
    filtered = current.astype(jnp.bfloat16).reshape(local_slots, cells)
    select = (assignment[:, None] == lax.iota(jnp.int32, total_slots)[None, :]).astype(jnp.float32)
    permuted = jnp.dot(select, rotation, precision=lax.Precision.HIGHEST)
    slot_rotation = jnp.dot(permuted, select.T, precision=lax.Precision.HIGHEST).astype(
        jnp.bfloat16
    )
    own_columns = lax.dynamic_slice_in_dim(slot_rotation, group * local_slots, local_slots, 1)
    shard_rows = lax.all_gather(filtered, "band", axis=0, tiled=True)
    margin = lax.dot_general(
        filtered, shard_rows, (((1,), (1,)), ((), ())), preferred_element_type=jnp.float32
    )
    gram_part = margin
    rotated_part = lax.dot_general(
        own_columns, shard_rows, (((0,), (0,)), ((), ())), preferred_element_type=jnp.float32
    )
    gram_part, rotated_flat = (gram_part, rotated_part)
    gram = lax.psum(gram_part, ("gx", "gyz")) / total_cells
    rotated = rotated_flat.reshape(local_slots, size_x, size_y, size_z)
    return (gram, rotated)


def solution(mesh):
    placed = (
        P("band", "gx", "gyz", None),
        P("gx", "gyz", None),
        P(None, "gx", "gyz", None),
        P(),
        P(),
        P(),
        P(),
        P(),
        P("band"),
    )
    return jax.shard_map(
        on_device,
        mesh=mesh,
        in_specs=placed,
        out_specs=(P("band", None), P("band", "gx", "gyz", None)),
        check_vma=False,
    )
```

profile of v0, /device:TPU:1, one launch (start us, length us, event | category | flops | bytes accessed | tf_op | source)
XLA Modules:
  0.0 743.6 jit_solution(973591448265603997)
XLA Ops:
  9.1 4.5 collective-permute-start.1
  17.2 3.4 multiply_convert_fusion.1
  20.7 3.3 fusion.1
  26.0 4.2 collective-permute-start.3
  30.2 3.2 collective-permute-done.2
  36.9 2.2 collective-permute-start.4
  39.1 3.3 collective-permute-start.5
  47.1 4.7 collective-permute-start.7
  59.6 5.5 collective-permute-start.9
  69.7 5.4 collective-permute-start.11
  75.1 3.0 collective-permute-done.10
  84.0 4.8 collective-permute-start.13
  93.4 5.8 collective-permute-start.15
  99.2 2.8 collective-permute-done.14
  108.0 4.8 collective-permute-start.17
  117.5 5.6 collective-permute-start.19
  123.1 3.0 collective-permute-done.18
  126.1 2.1 select_maximum_fusion.12
  131.5 4.8 collective-permute-start.21
  140.9 5.6 collective-permute-start.23
  146.6 3.0 collective-permute-done.22
  155.3 4.8 collective-permute-start.25
  164.8 5.6 collective-permute-start.27
  170.4 3.0 collective-permute-done.26
  173.4 2.1 select_maximum_fusion.4
  178.8 4.8 collective-permute-start.29
  188.2 5.6 collective-permute-start.31
  193.9 3.0 collective-permute-done.30
  196.9 2.1 select_maximum_fusion
  202.6 58.1 %all-gather.2.cloned.1.call-done = bf16[256,4096]{1,0:T(8,128)(2,1)} async-done(((bf16[64,4096]{1,0:T(8,128)(2,1)}), bf16[256,4096]{1,0:T(8,128)(2,1)}) %all-gather.2.cloned.1.call-update) | async-done | bytes 2097168 | tf_op jit(solution)/shard_map/all_gather | solution.py:89
  260.7 3.2 fusion.91
  265.5 469.7 %all-reduce.10.cloned.1.call-done = f32[64,256]{1,0:T(8,128)} async-done(((f32[64,256]{1,0:T(8,128)}), f32[64,256]{1,0:T(8,128)}) %all-reduce.10.cloned.1.call-update) | async-done | bytes 65552 | tf_op jit(solution)/shard_map/psum | solution.py:98
  (101 shorter events, 81.5 us)
Async XLA Ops:
  7.2 253.5 %all-gather.2.cloned.1.call-start = ((), (), s32[]{:S(2)}) async-start(), calls=%async_computation | async-start | bytes 2621440 | tf_op jit(solution)/shard_map/all_gather | solution.py:89
  9.1 14.9 %collective-permute-start.1 = (f32[64,1,8,128]{3,0,2,1:T(8,128)S(1)}, f32[64,1,8,128]{3,0,2,1:T(8,128)S(1)}, u32[]{:S(2)}, u32[]{:S(2)}) collective-permute-start(f32[64,1,8,128]{3,0,2,1:T(8,128)S(1)} %get-tuple-element.37), channel_id=1, source_target_pairs={{0,32},{32,64},{64,96},{96,128},{128,160},{160,192},{192,224},{1,3... | collective-permute-start | bytes 786440 | tf_op jit(solution)/shard_map/ppermute | solution.py:19
  13.7 11.0 %collective-permute-start = (f32[64,1,8,128]{3,0,2,1:T(8,128)S(1)}, f32[64,1,8,128]{3,0,2,1:T(8,128)S(1)}, u32[]{:S(2)}, u32[]{:S(2)}) collective-permute-start(f32[64,1,8,128]{3,0,2,1:T(8,128)S(1)} %get-tuple-element.36), channel_id=1, source_target_pairs={{32,0},{64,32},{96,64},{128,96},{160,128},{192,160},{224,192},{33,... | collective-permute-start | bytes 786440 | tf_op jit(solution)/shard_map/ppermute | solution.py:22
  24.7 8.7 %collective-permute-start.2 = (f32[64,6,1,128]{3,0,2,1:T(8,128)S(1)}, f32[64,6,1,128]{3,0,2,1:T(8,128)S(1)}, u32[]{:S(2)}, u32[]{:S(2)}) collective-permute-start(f32[64,6,1,128]{3,0,2,1:T(8,128)S(1)} %get-tuple-element.21), channel_id=1, source_target_pairs={{4,0},{8,4},{12,8},{16,12},{20,16},{24,20},{28,24},{5,1},{9,5},{13... | collective-permute-start | bytes 589832 | tf_op jit(solution)/shard_map/ppermute | solution.py:22
  26.0 8.9 %collective-permute-start.3 = (f32[64,6,1,128]{3,0,2,1:T(8,128)S(1)}, f32[64,6,1,128]{3,0,2,1:T(8,128)S(1)}, u32[]{:S(2)}, u32[]{:S(2)}) collective-permute-start(f32[64,6,1,128]{3,0,2,1:T(8,128)S(1)} %get-tuple-element.20), channel_id=1, source_target_pairs={{0,4},{4,8},{8,12},{12,16},{16,20},{20,24},{24,28},{1,5},{5,9},{9,... | collective-permute-start | bytes 589832 | tf_op jit(solution)/shard_map/ppermute | solution.py:19
  36.9 7.7 %collective-permute-start.4 = (f32[64,1,8,128]{3,0,2,1:T(8,128)S(1)}, f32[64,1,8,128]{3,0,2,1:T(8,128)S(1)}, u32[]{:S(2)}, u32[]{:S(2)}) collective-permute-start(f32[64,1,8,128]{3,0,2,1:T(8,128)S(1)} %get-tuple-element.35), channel_id=1, source_target_pairs={{32,0},{64,32},{96,64},{128,96},{160,128},{192,160},{224,192},{33,... | collective-permute-start | bytes 786440 | tf_op jit(solution)/shard_map/ppermute | solution.py:22
  47.1 7.3 collective-permute-start.7
  57.7 9.5 %collective-permute-start.8 = (f32[64,1,8,128]{3,0,2,1:T(8,128)S(1)}, f32[64,1,8,128]{3,0,2,1:T(8,128)S(1)}, u32[]{:S(2)}, u32[]{:S(2)}) collective-permute-start(f32[64,1,8,128]{3,0,2,1:T(8,128)S(1)} %get-tuple-element.33), channel_id=1, source_target_pairs={{32,0},{64,32},{96,64},{128,96},{160,128},{192,160},{224,192},{33,... | collective-permute-start | bytes 786440 | tf_op jit(solution)/shard_map/ppermute | solution.py:22
  59.6 8.8 %collective-permute-start.9 = (f32[64,1,8,128]{3,0,2,1:T(8,128)S(1)}, f32[64,1,8,128]{3,0,2,1:T(8,128)S(1)}, u32[]{:S(2)}, u32[]{:S(2)}) collective-permute-start(f32[64,1,8,128]{3,0,2,1:T(8,128)S(1)} %get-tuple-element.32), channel_id=1, source_target_pairs={{0,32},{32,64},{64,96},{96,128},{128,160},{160,192},{192,224},{1,3... | collective-permute-start | bytes 786440 | tf_op jit(solution)/shard_map/ppermute | solution.py:19
  68.4 9.7 %collective-permute-start.10 = (f32[64,6,1,128]{3,0,2,1:T(8,128)S(1)}, f32[64,6,1,128]{3,0,2,1:T(8,128)S(1)}, u32[]{:S(2)}, u32[]{:S(2)}) collective-permute-start(f32[64,6,1,128]{3,0,2,1:T(8,128)S(1)} %get-tuple-element.17), channel_id=1, source_target_pairs={{4,0},{8,4},{12,8},{16,12},{20,16},{24,20},{28,24},{5,1},{9,5},{13... | collective-permute-start | bytes 589832 | tf_op jit(solution)/shard_map/ppermute | solution.py:22
  69.7 8.4 %collective-permute-start.11 = (f32[64,6,1,128]{3,0,2,1:T(8,128)S(1)}, f32[64,6,1,128]{3,0,2,1:T(8,128)S(1)}, u32[]{:S(2)}, u32[]{:S(2)}) collective-permute-start(f32[64,6,1,128]{3,0,2,1:T(8,128)S(1)} %get-tuple-element.16), channel_id=1, source_target_pairs={{0,4},{4,8},{8,12},{12,16},{16,20},{20,24},{24,28},{1,5},{5,9},{9,... | collective-permute-start | bytes 589832 | tf_op jit(solution)/shard_map/ppermute | solution.py:19
  82.0 8.9 %collective-permute-start.12 = (f32[64,1,8,128]{3,0,2,1:T(8,128)S(1)}, f32[64,1,8,128]{3,0,2,1:T(8,128)S(1)}, u32[]{:S(2)}, u32[]{:S(2)}) collective-permute-start(f32[64,1,8,128]{3,0,2,1:T(8,128)S(1)} %get-tuple-element.31), channel_id=1, source_target_pairs={{32,0},{64,32},{96,64},{128,96},{160,128},{192,160},{224,192},{33,... | collective-permute-start | bytes 786440 | tf_op jit(solution)/shard_map/ppermute | solution.py:22
  84.0 8.1 %collective-permute-start.13 = (f32[64,1,8,128]{3,0,2,1:T(8,128)S(1)}, f32[64,1,8,128]{3,0,2,1:T(8,128)S(1)}, u32[]{:S(2)}, u32[]{:S(2)}) collective-permute-start(f32[64,1,8,128]{3,0,2,1:T(8,128)S(1)} %get-tuple-element.30), channel_id=1, source_target_pairs={{0,32},{32,64},{64,96},{96,128},{128,160},{160,192},{192,224},{1,3... | collective-permute-start | bytes 786440 | tf_op jit(solution)/shard_map/ppermute | solution.py:19
  92.1 10.0 %collective-permute-start.14 = (f32[64,6,1,128]{3,0,2,1:T(8,128)S(1)}, f32[64,6,1,128]{3,0,2,1:T(8,128)S(1)}, u32[]{:S(2)}, u32[]{:S(2)}) collective-permute-start(f32[64,6,1,128]{3,0,2,1:T(8,128)S(1)} %get-tuple-element.15), channel_id=1, source_target_pairs={{4,0},{8,4},{12,8},{16,12},{20,16},{24,20},{28,24},{5,1},{9,5},{13... | collective-permute-start | bytes 589832 | tf_op jit(solution)/shard_map/ppermute | solution.py:22
  93.4 8.7 %collective-permute-start.15 = (f32[64,6,1,128]{3,0,2,1:T(8,128)S(1)}, f32[64,6,1,128]{3,0,2,1:T(8,128)S(1)}, u32[]{:S(2)}, u32[]{:S(2)}) collective-permute-start(f32[64,6,1,128]{3,0,2,1:T(8,128)S(1)} %get-tuple-element.14), channel_id=1, source_target_pairs={{0,4},{4,8},{8,12},{12,16},{16,20},{20,24},{24,28},{1,5},{5,9},{9,... | collective-permute-start | bytes 589832 | tf_op jit(solution)/shard_map/ppermute | solution.py:19
  106.1 8.9 %collective-permute-start.16 = (f32[64,1,8,128]{3,0,2,1:T(8,128)S(1)}, f32[64,1,8,128]{3,0,2,1:T(8,128)S(1)}, u32[]{:S(2)}, u32[]{:S(2)}) collective-permute-start(f32[64,1,8,128]{3,0,2,1:T(8,128)S(1)} %get-tuple-element.29), channel_id=1, source_target_pairs={{32,0},{64,32},{96,64},{128,96},{160,128},{192,160},{224,192},{33,... | collective-permute-start | bytes 786440 | tf_op jit(solution)/shard_map/ppermute | solution.py:22
  108.0 8.1 %collective-permute-start.17 = (f32[64,1,8,128]{3,0,2,1:T(8,128)S(1)}, f32[64,1,8,128]{3,0,2,1:T(8,128)S(1)}, u32[]{:S(2)}, u32[]{:S(2)}) collective-permute-start(f32[64,1,8,128]{3,0,2,1:T(8,128)S(1)} %get-tuple-element.28), channel_id=1, source_target_pairs={{0,32},{32,64},{64,96},{96,128},{128,160},{160,192},{192,224},{1,3... | collective-permute-start | bytes 786440 | tf_op jit(solution)/shard_map/ppermute | solution.py:19
  116.2 10.0 %collective-permute-start.18 = (f32[64,6,1,128]{3,0,2,1:T(8,128)S(1)}, f32[64,6,1,128]{3,0,2,1:T(8,128)S(1)}, u32[]{:S(2)}, u32[]{:S(2)}) collective-permute-start(f32[64,6,1,128]{3,0,2,1:T(8,128)S(1)} %get-tuple-element.13), channel_id=1, source_target_pairs={{4,0},{8,4},{12,8},{16,12},{20,16},{24,20},{28,24},{5,1},{9,5},{13... | collective-permute-start | bytes 589832 | tf_op jit(solution)/shard_map/ppermute | solution.py:22
  117.5 8.7 %collective-permute-start.19 = (f32[64,6,1,128]{3,0,2,1:T(8,128)S(1)}, f32[64,6,1,128]{3,0,2,1:T(8,128)S(1)}, u32[]{:S(2)}, u32[]{:S(2)}) collective-permute-start(f32[64,6,1,128]{3,0,2,1:T(8,128)S(1)} %get-tuple-element.12), channel_id=1, source_target_pairs={{0,4},{4,8},{8,12},{12,16},{16,20},{20,24},{24,28},{1,5},{5,9},{9,... | collective-permute-start | bytes 589832 | tf_op jit(solution)/shard_map/ppermute | solution.py:19
  129.6 8.9 %collective-permute-start.20 = (f32[64,1,8,128]{3,0,2,1:T(8,128)S(1)}, f32[64,1,8,128]{3,0,2,1:T(8,128)S(1)}, u32[]{:S(2)}, u32[]{:S(2)}) collective-permute-start(f32[64,1,8,128]{3,0,2,1:T(8,128)S(1)} %get-tuple-element.27), channel_id=1, source_target_pairs={{32,0},{64,32},{96,64},{128,96},{160,128},{192,160},{224,192},{33,... | collective-permute-start | bytes 786440 | tf_op jit(solution)/shard_map/ppermute | solution.py:22
  131.5 8.1 %collective-permute-start.21 = (f32[64,1,8,128]{3,0,2,1:T(8,128)S(1)}, f32[64,1,8,128]{3,0,2,1:T(8,128)S(1)}, u32[]{:S(2)}, u32[]{:S(2)}) collective-permute-start(f32[64,1,8,128]{3,0,2,1:T(8,128)S(1)} %get-tuple-element.26), channel_id=1, source_target_pairs={{0,32},{32,64},{64,96},{96,128},{128,160},{160,192},{192,224},{1,3... | collective-permute-start | bytes 786440 | tf_op jit(solution)/shard_map/ppermute | solution.py:19
  139.6 10.0 %collective-permute-start.22 = (f32[64,6,1,128]{3,0,2,1:T(8,128)S(1)}, f32[64,6,1,128]{3,0,2,1:T(8,128)S(1)}, u32[]{:S(2)}, u32[]{:S(2)}) collective-permute-start(f32[64,6,1,128]{3,0,2,1:T(8,128)S(1)} %get-tuple-element.11), channel_id=1, source_target_pairs={{4,0},{8,4},{12,8},{16,12},{20,16},{24,20},{28,24},{5,1},{9,5},{13... | collective-permute-start | bytes 589832 | tf_op jit(solution)/shard_map/ppermute | solution.py:22
  140.9 8.7 %collective-permute-start.23 = (f32[64,6,1,128]{3,0,2,1:T(8,128)S(1)}, f32[64,6,1,128]{3,0,2,1:T(8,128)S(1)}, u32[]{:S(2)}, u32[]{:S(2)}) collective-permute-start(f32[64,6,1,128]{3,0,2,1:T(8,128)S(1)} %get-tuple-element.10), channel_id=1, source_target_pairs={{0,4},{4,8},{8,12},{12,16},{16,20},{20,24},{24,28},{1,5},{5,9},{9,... | collective-permute-start | bytes 589832 | tf_op jit(solution)/shard_map/ppermute | solution.py:19
  153.4 8.9 %collective-permute-start.24 = (f32[64,1,8,128]{3,0,2,1:T(8,128)S(1)}, f32[64,1,8,128]{3,0,2,1:T(8,128)S(1)}, u32[]{:S(2)}, u32[]{:S(2)}) collective-permute-start(f32[64,1,8,128]{3,0,2,1:T(8,128)S(1)} %get-tuple-element.25), channel_id=1, source_target_pairs={{32,0},{64,32},{96,64},{128,96},{160,128},{192,160},{224,192},{33,... | collective-permute-start | bytes 786440 | tf_op jit(solution)/shard_map/ppermute | solution.py:22
  155.3 8.1 %collective-permute-start.25 = (f32[64,1,8,128]{3,0,2,1:T(8,128)S(1)}, f32[64,1,8,128]{3,0,2,1:T(8,128)S(1)}, u32[]{:S(2)}, u32[]{:S(2)}) collective-permute-start(f32[64,1,8,128]{3,0,2,1:T(8,128)S(1)} %get-tuple-element.24), channel_id=1, source_target_pairs={{0,32},{32,64},{64,96},{96,128},{128,160},{160,192},{192,224},{1,3... | collective-permute-start | bytes 786440 | tf_op jit(solution)/shard_map/ppermute | solution.py:19
  163.5 10.0 %collective-permute-start.26 = (f32[64,6,1,128]{3,0,2,1:T(8,128)S(1)}, f32[64,6,1,128]{3,0,2,1:T(8,128)S(1)}, u32[]{:S(2)}, u32[]{:S(2)}) collective-permute-start(f32[64,6,1,128]{3,0,2,1:T(8,128)S(1)} %get-tuple-element.9), channel_id=1, source_target_pairs={{4,0},{8,4},{12,8},{16,12},{20,16},{24,20},{28,24},{5,1},{9,5},{13... | collective-permute-start | bytes 589832 | tf_op jit(solution)/shard_map/ppermute | solution.py:22
  164.8 8.7 %collective-permute-start.27 = (f32[64,6,1,128]{3,0,2,1:T(8,128)S(1)}, f32[64,6,1,128]{3,0,2,1:T(8,128)S(1)}, u32[]{:S(2)}, u32[]{:S(2)}) collective-permute-start(f32[64,6,1,128]{3,0,2,1:T(8,128)S(1)} %get-tuple-element.8), channel_id=1, source_target_pairs={{0,4},{4,8},{8,12},{12,16},{16,20},{20,24},{24,28},{1,5},{5,9},{9,... | collective-permute-start | bytes 589832 | tf_op jit(solution)/shard_map/ppermute | solution.py:19
  176.9 8.9 %collective-permute-start.28 = (f32[64,1,8,128]{3,0,2,1:T(8,128)S(1)}, f32[64,1,8,128]{3,0,2,1:T(8,128)S(1)}, u32[]{:S(2)}, u32[]{:S(2)}) collective-permute-start(f32[64,1,8,128]{3,0,2,1:T(8,128)S(1)} %get-tuple-element.23), channel_id=1, source_target_pairs={{32,0},{64,32},{96,64},{128,96},{160,128},{192,160},{224,192},{33,... | collective-permute-start | bytes 786440 | tf_op jit(solution)/shard_map/ppermute | solution.py:22
  178.8 8.1 %collective-permute-start.29 = (f32[64,1,8,128]{3,0,2,1:T(8,128)S(1)}, f32[64,1,8,128]{3,0,2,1:T(8,128)S(1)}, u32[]{:S(2)}, u32[]{:S(2)}) collective-permute-start(f32[64,1,8,128]{3,0,2,1:T(8,128)S(1)} %get-tuple-element.22), channel_id=1, source_target_pairs={{0,32},{32,64},{64,96},{96,128},{128,160},{160,192},{192,224},{1,3... | collective-permute-start | bytes 786440 | tf_op jit(solution)/shard_map/ppermute | solution.py:19
  186.9 10.0 %collective-permute-start.30 = (f32[64,6,1,128]{3,0,2,1:T(8,128)S(1)}, f32[64,6,1,128]{3,0,2,1:T(8,128)S(1)}, u32[]{:S(2)}, u32[]{:S(2)}) collective-permute-start(f32[64,6,1,128]{3,0,2,1:T(8,128)S(1)} %get-tuple-element.7), channel_id=1, source_target_pairs={{4,0},{8,4},{12,8},{16,12},{20,16},{24,20},{28,24},{5,1},{9,5},{13... | collective-permute-start | bytes 589832 | tf_op jit(solution)/shard_map/ppermute | solution.py:22
  188.2 8.7 %collective-permute-start.31 = (f32[64,6,1,128]{3,0,2,1:T(8,128)S(1)}, f32[64,6,1,128]{3,0,2,1:T(8,128)S(1)}, u32[]{:S(2)}, u32[]{:S(2)}) collective-permute-start(f32[64,6,1,128]{3,0,2,1:T(8,128)S(1)} %get-tuple-element.6), channel_id=1, source_target_pairs={{0,4},{4,8},{8,12},{12,16},{16,20},{20,24},{24,28},{1,5},{5,9},{9,... | collective-permute-start | bytes 589832 | tf_op jit(solution)/shard_map/ppermute | solution.py:19
  201.8 533.4 %all-reduce.10.cloned.1.call-start = ((), (), s32[]{:S(2)}) async-start(), calls=%async_computation.1 | async-start | bytes 131072 | tf_op jit(solution)/shard_map/psum | solution.py:98
  (8 other events, 227.4 us)
Sparse Core Ops, SparseCore 0:
  201.9 58.6 all-gather.1
  264.0 471.2 all-reduce.9
where the time goes:
time: 752 us; the launch traced here: 744 us
  waiting for transfers between devices  576 us (77%)
  starting transfers between devices  106 us (14%)
  other arithmetic  28.6 us (4%)
  between operations  14.7 us (2%)
  matrix products  11 us (1%)
    psum x1, waiting for transfers between devices, on_device(): gram = lax.psum(gram_part, ('gx', 'gyz')) / total_cells  470 us
    ppermute x16, starting transfers between devices, with_halo(): lax.ppermute(lax.slice_in_dim(block, block.shape[dim] - width, None, axis...  80 us
    all_gather x1, waiting for transfers between devices, on_device(): shard_rows = lax.all_gather(filtered, 'band', axis=0, tiled=True)  58.1 us
    ppermute x16, waiting for transfers between devices, with_halo(): lax.ppermute(lax.slice_in_dim(block, 0, width, axis=dim), axis, backward)  37 us
    ppermute x16, starting transfers between devices, with_halo(): lax.ppermute(lax.slice_in_dim(block, 0, width, axis=dim), axis, backward)  26 us
    concatenate x15, other arithmetic, with_halo(): block = jnp.concatenate([low, block, high], axis=dim)  16.2 us
  transfers between devices with their start and end apart: 34, of which 26 were waited for; matrix products, arithmetic and copies ran while one was open for 2% of the time, Pallas kernels for 0%

commit v1 on v0

v1 whole, which is shorter than its diff:
```python
import jax
import jax.numpy as jnp
from jax import lax
from jax.experimental import pallas as pl
from jax.experimental.pallas import tpu as pltpu
from jax.sharding import PartitionSpec as P

DEG = 8


LOWER_EDGE = 2.0
CUT_EDGE = 3.0
UPPER_EDGE = 9.5


def coefficients(count):
    half_width = (UPPER_EDGE - CUT_EDGE) / 2.0
    centre = (UPPER_EDGE + CUT_EDGE) / 2.0
    first = half_width / (LOWER_EDGE - centre)
    factors = [(first / half_width, 0.0)]
    sigma = first
    for rounds in range(1, count):
        updated = 1.0 / (2.0 / first - sigma)
        factors.append((2.0 * updated / half_width, sigma * updated))
        sigma = updated
    return (factors, centre)


def network(cell_features, w_first, w_hidden, w_last):
    feature_count = cell_features.shape[0]
    flattened = cell_features.reshape(feature_count, -1)
    hidden = jax.nn.silu(jnp.dot(w_first, flattened, preferred_element_type=jnp.float32)).astype(
        jnp.bfloat16
    )
    hidden = jax.nn.silu(jnp.dot(w_hidden[0], hidden, preferred_element_type=jnp.float32)).astype(
        jnp.bfloat16
    )
    values = jnp.tanh(jnp.dot(w_last[None, :], hidden, preferred_element_type=jnp.float32)[0])
    return values.reshape(cell_features.shape[1:])


NX, NY, NZ = 32, 64, 128
PAD = 8


def filter_kernel(info, taken, other, out, field, shifted):
    factors, centre = coefficients(DEG)
    core = info[0]
    degree = info[1]
    edge = jnp.zeros((NY + 2 * PAD, NZ), jnp.float32)
    rim = jnp.zeros((PAD, NZ), jnp.float32)
    for which in range(2):
        field[which, 0] = edge
        field[which, NX + 1] = edge

    def load(plane, carry):
        outer = lax.div(plane, 4)
        inner = lax.rem(plane, 4)
        half = lax.div(inner, 2)
        place = lax.rem(inner, 2)
        for which in range(2):
            field[which, plane + 1, 0:PAD] = rim
            field[which, plane + 1, PAD + NY :] = rim
        for run in range(8):
            rows = slice(PAD + 8 * run, PAD + 8 * run + 8)
            block = taken[outer * 8 + run, inner]
            field[0, plane + 1, rows] = block
            field[1, plane + 1, rows] = block
            own = taken[outer * 8 + run, 4 + place]
            far = other[outer * 8 + run, place]
            value = jnp.where(half == core, own, far)
            shifted[plane, 8 * run : 8 * run + 8] = value + (3.0 - centre)
        return carry

    lax.fori_loop(0, NX, load, 0)
    lane = lax.broadcasted_iota(jnp.int32, (NY, NZ), 1)
    not_first = lane > 0
    not_last = lane < NZ - 1
    for rounds in range(DEG):
        scale_new, scale_old = factors[rounds]
        now = rounds % 2
        then = 1 - now

        @pl.when(rounds < degree)
        def _():
            def step(plane, carry):
                x = plane + 1
                here = field[now, x, PAD : PAD + NY]
                beside = field[now, x - 1, PAD : PAD + NY] + field[now, x + 1, PAD : PAD + NY]
                beside += (
                    field[now, x, PAD - 1 : PAD + NY - 1] + field[now, x, PAD + 1 : PAD + NY + 1]
                )
                beside += jnp.where(not_first, pltpu.roll(here, 1, 1), 0.0)
                beside += jnp.where(not_last, pltpu.roll(here, NZ - 1, 1), 0.0)
                fresh = scale_new * (shifted[plane] * here - 0.5 * beside)
                if scale_old != 0.0:
                    fresh -= scale_old * field[then, x, PAD : PAD + NY]
                field[then, x, PAD : PAD + NY] = fresh
                return carry

            lax.fori_loop(0, NX, step, 0)

    last = lax.rem(degree, 2)

    def store(plane, carry):
        out[lax.rem(plane, 4), lax.div(plane, 4)] = field[last, plane + 1, PAD : PAD + NY].astype(
            jnp.bfloat16
        )
        return carry

    lax.fori_loop(0, NX, store, 0)


def run_filter(info, taken, other):
    vmem = pl.BlockSpec(memory_space=pltpu.VMEM)
    return pl.pallas_call(
        filter_kernel,
        out_shape=jax.ShapeDtypeStruct((4, 8, NY, NZ), jnp.bfloat16),
        in_specs=[pl.BlockSpec(memory_space=pltpu.SMEM), vmem, vmem],
        out_specs=vmem,
        scratch_shapes=[
            pltpu.VMEM((2, NX + 2, NY + 2 * PAD, NZ), jnp.float32),
            pltpu.VMEM((NX, NY, NZ), jnp.float32),
        ],
        compiler_params=pltpu.CompilerParams(vmem_limit_bytes=24 * 1024 * 1024),
        cost_estimate=pl.CostEstimate(
            flops=8 * 16 * NX * NY * NZ, bytes_accessed=3 * 1024 * 1024, transcendentals=0
        ),
    )(info, taken, other)


def reduce_over(value, axis, step, count):
    size = lax.axis_size(axis)
    total = value
    for shift in range(1, count):
        pairs = []
        for i in range(size):
            place = (i // step) % count
            pairs.append((i, i + (((place + shift) % count) - place) * step))
        total = total + lax.ppermute(value, axis, pairs)
    return total


def on_device(
    orbitals, v_local, features, w_first, w_hidden, w_last, rotation, assignment, degrees
):
    band = lax.axis_index("band")
    gx = lax.axis_index("gx")
    gyz = lax.axis_index("gyz")
    total_slots = rotation.shape[0]
    local_slots, size_x, size_y, size_z = orbitals.shape
    total_cells = float(NX * NY * NZ)

    potential = v_local + network(features, w_first, w_hidden, w_last)
    halves = potential.reshape(1, 2, 1, 2, size_y, size_z)
    halves = jnp.broadcast_to(halves, (4, 2, 8, 2, size_y, size_z)).reshape(64, 2, size_y, size_z)
    message = jnp.concatenate([orbitals, halves], axis=1)
    taken = lax.all_to_all(message, ("gx", "gyz"), 0, 0, tiled=True)
    other = lax.ppermute(taken[:, 4:], "gx", [(i, i ^ 1) for i in range(8)])
    degree = lax.dynamic_index_in_dim(degrees, gx * 8 + gyz, 0, keepdims=False)
    info = jnp.stack([lax.rem(gx, 2), degree]).astype(jnp.int32)
    filtered = run_filter(info, taken, other)

    select = (assignment[:, None] == lax.iota(jnp.int32, total_slots)[None, :]).astype(jnp.bfloat16)
    permuted = jnp.dot(
        select, rotation.astype(jnp.bfloat16), preferred_element_type=jnp.float32
    ).astype(jnp.bfloat16)
    slot_rotation = jnp.dot(permuted, select.T, preferred_element_type=jnp.float32).astype(
        jnp.bfloat16
    )

    panel = lax.all_to_all(
        filtered.reshape(256, 8, 128), ("band", "gx", "gyz"), 0, 0, tiled=True
    ).reshape(256, 1024)
    margin = lax.dot_general(
        panel, panel, (((1,), (1,)), ((), ())), preferred_element_type=jnp.float32
    )
    turned = lax.dot_general(
        slot_rotation, panel, (((0,), (0,)), ((), ())), preferred_element_type=jnp.float32
    ).astype(jnp.bfloat16)

    rows = margin.reshape(4, local_slots, total_slots)
    gram = lax.dynamic_index_in_dim(rows, band, 0, keepdims=False)
    for shift in range(1, 4):
        piece = lax.dynamic_index_in_dim(rows, lax.rem(band + shift, 4), 0, keepdims=False)
        gram = gram + lax.ppermute(piece, "band", [(i, (i + shift) % 4) for i in range(4)])
    gram = reduce_over(gram, "gx", 1, 2)
    gram = reduce_over(gram, "gyz", 1, 2)
    gram = reduce_over(gram, "gx", 2, 4)
    gram = reduce_over(gram, "gyz", 2, 4) / total_cells

    back = lax.all_to_all(turned.reshape(4, local_slots, 1024), "band", 0, 0, tiled=True)
    rotated = jnp.swapaxes(back, 0, 1).reshape(local_slots, size_x, size_y, size_z)
    return (gram, rotated.astype(jnp.float32))


def solution(mesh):
    placed = (
        P("band", "gx", "gyz", None),
        P("gx", "gyz", None),
        P(None, "gx", "gyz", None),
        P(),
        P(),
        P(),
        P(),
        P(),
        P("band"),
    )
    return jax.shard_map(
        on_device,
        mesh=mesh,
        in_specs=placed,
        out_specs=(P("band", None), P("band", "gx", "gyz", None)),
        check_vma=False,
    )
```

time: 752 us -> 140 us (0.19)
  waiting for transfers between devices: 576 us -> 37.3 us
  starting transfers between devices: 106 us -> 35.2 us
  blocking collectives: 0 us -> 33.7 us
  other arithmetic: 28.6 us -> 1.53 us
  Pallas kernels: 0 us -> 19.4 us
  between operations: 14.7 us -> 0.87 us
    psum x1 -> x0, waiting for transfers between devices: 470 us -> none  [on_device(): gram = lax.psum(gram_part, ('gx', 'gyz')) / total_cells]
    ppermute x32 -> x12, starting transfers between devices: 106 us -> 14.4 us  [the longest x8 10.5 us: reduce_over(): total = total + lax.ppermute(value, axis, pairs)]
    all_gather x1 -> x0, waiting for transfers between devices: 58.1 us -> none  [on_device(): shard_rows = lax.all_gather(filtered, 'band', axis=0, tiled=True)]
    all_to_all x0 -> x1, blocking collectives: none -> 33.7 us  [on_device(): taken = lax.all_to_all(message, ('gx', 'gyz'), 0, 0, tiled=True)]
    ppermute x32 -> x12, waiting for transfers between devices: 48.2 us -> 16.5 us  [the longest x8 15.7 us: reduce_over(): total = total + lax.ppermute(value, axis, pairs)]
    all_to_all x0 -> x2, starting transfers between devices: none -> 20.8 us  [the longest x1 15.4 us: on_device(): lax.all_to_all(filtered.reshape(256, 8, 128), ('band', 'gx', 'gyz'), 0, 0...]
    all_to_all x0 -> x2, waiting for transfers between devices: none -> 20.8 us  [the longest x1 20.8 us: on_device(): lax.all_to_all(filtered.reshape(256, 8, 128), ('band', 'gx', 'gyz'), 0, 0...]
    pallas_call x0 -> x1, Pallas kernels: none -> 19.4 us  [run_filter(): pl.pallas_call(filter_kernel, out_shape=jax.ShapeDtypeStruct((4, 8, NY, N...]
  transfers between devices with their start and end apart: 34 -> 14, of which waited for: 26 -> 10; matrix products, arithmetic and copies ran while one was open for 2% -> 3% of each run, Pallas kernels for 0% -> 0%
where the time goes in v1:
time: 140 us; the launch traced here: 138 us
  waiting for transfers between devices  37.3 us (27%)
  starting transfers between devices  35.2 us (25%)
  blocking collectives  33.7 us (24%)
  Pallas kernels  19.4 us (14%)
  matrix products  5.71 us (4%)
  local copies, waits for them, and re-layouts  4.05 us (3%)
  other arithmetic  1.53 us (1%)
    all_to_all x1, blocking collectives, on_device(): taken = lax.all_to_all(message, ('gx', 'gyz'), 0, 0, tiled=True)  33.7 us
    all_to_all x1, waiting for transfers between devices, on_device(): lax.all_to_all(filtered.reshape(256, 8, 128), ('band', 'gx', 'gyz'), 0, 0...  20.8 us
    pallas_call x1, Pallas kernels, run_filter(): pl.pallas_call(filter_kernel, out_shape=jax.ShapeDtypeStruct((4, 8, NY, N...  19.4 us
    ppermute x8, waiting for transfers between devices, reduce_over(): total = total + lax.ppermute(value, axis, pairs)  15.7 us
    all_to_all x1, starting transfers between devices, on_device(): lax.all_to_all(filtered.reshape(256, 8, 128), ('band', 'gx', 'gyz'), 0, 0...  15.4 us
    ppermute x8, starting transfers between devices, reduce_over(): total = total + lax.ppermute(value, axis, pairs)  10.5 us
    all_to_all x1, starting transfers between devices, on_device(): lax.all_to_all(turned.reshape(4, local_slots, 1024), 'band', 0, 0, tiled=...  5.46 us
    ppermute x3, starting transfers between devices, on_device(): lax.ppermute(piece, 'band', [(i, (i + shift) % 4) for i in range(4)])  3.62 us
  transfers between devices with their start and end apart: 14, of which 10 were waited for; matrix products, arithmetic and copies ran while one was open for 3% of the time, Pallas kernels for 0%

profile of v1, /device:TPU:1, one launch (start us, length us, event | category | flops | bytes accessed | tf_op | source)
XLA Modules:
  0.0 137.8 jit_solution(4189949962691647607)
XLA Ops:
  0.6 0.7 reshape.41
  1.3 0.9 pad.4
  2.3 2.1 %multiply_convert_fusion.1 = bf16[256,4096]{1,0:T(8,128)(2,1)S(1)} fusion(bf16[256,11]{0,1:T(8,128)(2,1)} %param.12, bf16[11,4096]{1,0:T(8,128)(2,1)S(1)} %bitcast.58), kind=kOutput, calls=%fused_computation.2 | convolution fusion | flops 28311552 | bytes 2192896 | tf_op jit(solution)/shard_map/dot_general | solution.py:32
  4.4 1.6 %fusion = f32[1,4096]{1,0:T(1,128)S(1)} fusion(bf16[256,1]{0,1:T(2,128)(2,1)S(1)} %reshape.41, bf16[256,4096]{1,0:T(8,128)(2,1)S(1)} %multiply_convert_fusion.1, bf16[1,256,256]{2,1,0:T(8,128)(2,1)S(1)} %copy-done), kind=kOutput, calls=%fused_computation.4 | convolution fusion | flops 544210944 | bytes 2245120 | tf_op jit(solution)/shard_map/dot_general | solution.py:38
  6.2 33.7 %all_to_all.15.taken = f32[64,6,8,128]{3,2,1,0:T(8,128)S(1)} all-to-all(f32[64,6,8,128]{3,2,1,0:T(8,128)S(1)} %pad_maximum_fusion), channel_id=1, replica_groups=mesh['gx'=8,'gyz'=8,'band'=4] {'gx','gyz'}, dimensions={0} | all-to-all | bytes 3145728 | tf_op jit(solution)/shard_map/all_to_all | solution.py:158
  40.2 0.6 dynamic_slice.17
  40.8 0.7 pad_add_fusion.info
  41.5 0.5 collective-permute-done.other
  42.0 19.4 %shard_map.104 = bf16[4,8,64,128]{3,2,1,0:T(8,128)(2,1)} custom-call(s32[2]{0:T(128)S(1)} %pad_add_fusion.info, f32[64,6,8,128]{3,2,1,0:T(8,128)S(1)} %all_to_all.15.taken, f32[64,2,8,128]{3,2,1,0:T(8,128)S(1)} %collective-permute-done.other), custom_call_target="tpu_custom_call" | custom-call | flops 33554432 | bytes 3145728 | tf_op jit(solution)/shard_map/pallas_call | solution.py:116
  61.4 15.4 %all-to-all-start.1 = ((bf16[256,8,128]{2,1,0:T(8,128)(2,1)}), bf16[256,8,128]{2,1,0:T(8,128)(2,1)S(1)}, u32[]{:S(2)}, u32[]{:S(2)}) async-start(bf16[256,8,128]{2,1,0:T(8,128)(2,1)} %bitcast.7), calls=%async_computation.1 | async-start | bytes 1048576 | tf_op jit(solution)/shard_map/all_to_all | solution.py:172
  77.1 20.8 %all-to-all-done.1 = bf16[256,8,128]{2,1,0:T(8,128)(2,1)S(1)} async-done(((bf16[256,8,128]{2,1,0:T(8,128)(2,1)}), bf16[256,8,128]{2,1,0:T(8,128)(2,1)S(1)}, u32[]{:S(2)}, u32[]{:S(2)}) %all-to-all-start.1) | async-done | bytes 524320 | tf_op jit(solution)/shard_map/all_to_all | solution.py:172
  98.4 0.3 fusion.12
  98.7 0.7 collective-permute-start.3
  99.4 2.9 %collective-permute-start.2 = (f32[64,256]{1,0:T(8,128)S(1)}, f32[64,256]{1,0:T(8,128)S(1)}, u32[]{:S(2)}, u32[]{:S(2)}) collective-permute-start(f32[64,256]{1,0:T(8,128)S(1)} %get-tuple-element.4), channel_id=1, source_target_pairs={{0,2},{1,3},{2,0},{3,1},{4,6},{5,7},{6,4},{7,5},{8,10},{9,11},{10,... | collective-permute-start | bytes 196616 | tf_op jit(solution)/shard_map/ppermute | solution.py:186
  102.4 1.5 %convolution_convert_fusion = bf16[256,1024]{1,0:T(8,128)(2,1)} fusion(bf16[256,256]{1,0:T(8,128)(2,1)S(1)} %convolution_convert_fusion.2, bf16[32,8,8,128]{3,2,1,0:T(8,128)(2,1)S(1)} %bitcast.53, s32[256]{0:T(256)S(1)} %copy-done.4), kind=kOutput, calls=%fused_computation.5 | convolution fusion | flops 168165376 | bytes 1180672 | tf_op jit(solution)/shard_map/dot_general | solution.py:178
  103.8 5.5 %all-to-all-start.2 = ((bf16[4,64,1024]{2,1,0:T(8,128)(2,1)}), bf16[4,64,1024]{2,1,0:T(8,128)(2,1)S(1)}, u32[]{:S(2)}, u32[]{:S(2)}) async-start(bf16[4,64,1024]{2,1,0:T(8,128)(2,1)} %bitcast.12), calls=%async_computation.2 | async-start | bytes 1048576 | tf_op jit(solution)/shard_map/all_to_all | solution.py:192
  109.3 0.4 collective-permute-done.1
  109.7 1.7 %collective-permute-start.4 = (f32[64,256]{1,0:T(8,128)S(1)}, f32[64,256]{1,0:T(8,128)S(1)}, u32[]{:S(2)}, u32[]{:S(2)}) collective-permute-start(f32[64,256]{1,0:T(8,128)S(1)} %fusion.10), channel_id=1, source_target_pairs={{0,32},{32,0},{64,96},{96,64},{128,160},{160,128},{192,224},{224,1... | collective-permute-start | bytes 196616 | tf_op jit(solution)/shard_map/ppermute | solution.py:140
  111.4 0.9 collective-permute-done.4
  112.3 2.0 %collective-permute-start.5 = (f32[64,256]{1,0:T(8,128)S(1)}, f32[64,256]{1,0:T(8,128)S(1)}, u32[]{:S(2)}, u32[]{:S(2)}) collective-permute-start(f32[64,256]{1,0:T(8,128)S(1)} %add.87), channel_id=1, source_target_pairs={{0,4},{4,0},{8,12},{12,8},{16,20},{20,16},{24,28},{28,24},{1,5},{5... | collective-permute-start | bytes 196616 | tf_op jit(solution)/shard_map/ppermute | solution.py:140
  114.3 6.7 %collective-permute-done.5 = f32[64,256]{1,0:T(8,128)S(1)} collective-permute-done((f32[64,256]{1,0:T(8,128)S(1)}, f32[64,256]{1,0:T(8,128)S(1)}, u32[]{:S(2)}, u32[]{:S(2)}) %collective-permute-start.5) | collective-permute-done | bytes 65568 | tf_op jit(solution)/shard_map/ppermute | solution.py:140
  121.0 2.9 %collective-permute-start.8 = (f32[64,256]{1,0:T(8,128)S(1)}, f32[64,256]{1,0:T(8,128)S(1)}, u32[]{:S(2)}, u32[]{:S(2)}) collective-permute-start(f32[64,256]{1,0:T(8,128)S(1)} %add.88), channel_id=1, source_target_pairs={{0,192},{32,224},{64,0},{96,32},{128,64},{160,96},{192,128},{224,1... | collective-permute-start | bytes 196616 | tf_op jit(solution)/shard_map/ppermute | solution.py:140
  123.9 1.0 collective-permute-start.7
  124.9 0.6 collective-permute-start.6
  125.5 3.0 %collective-permute-done.7 = f32[64,256]{1,0:T(8,128)S(1)} collective-permute-done((f32[64,256]{1,0:T(8,128)S(1)}, f32[64,256]{1,0:T(8,128)S(1)}, u32[]{:S(2)}, u32[]{:S(2)}) %collective-permute-start.7) | collective-permute-done | bytes 65568 | tf_op jit(solution)/shard_map/ppermute | solution.py:140
  128.5 0.7 collective-permute-done.6
  129.4 2.3 %collective-permute-start.10 = (f32[64,256]{1,0:T(8,128)S(1)}, f32[64,256]{1,0:T(8,128)S(1)}, u32[]{:S(2)}, u32[]{:S(2)}) collective-permute-start(f32[64,256]{1,0:T(8,128)S(1)} %add_add_fusion), channel_id=1, source_target_pairs={{0,16},{4,20},{8,24},{12,28},{16,0},{20,4},{24,8},{28,12},{1,17},{... | collective-permute-start | bytes 196616 | tf_op jit(solution)/shard_map/ppermute | solution.py:140
  131.6 0.8 collective-permute-done.11
  132.5 1.6 %collective-permute-done.10 = f32[64,256]{1,0:T(8,128)S(1)} collective-permute-done((f32[64,256]{1,0:T(8,128)S(1)}, f32[64,256]{1,0:T(8,128)S(1)}, u32[]{:S(2)}, u32[]{:S(2)}) %collective-permute-start.10) | collective-permute-done | bytes 65568 | tf_op jit(solution)/shard_map/ppermute | solution.py:140
  134.1 1.9 %collective-permute-done.9 = f32[64,256]{1,0:T(8,128)S(1)} collective-permute-done((f32[64,256]{1,0:T(8,128)S(1)}, f32[64,256]{1,0:T(8,128)S(1)}, u32[]{:S(2)}, u32[]{:S(2)}) %collective-permute-start.9) | collective-permute-done | bytes 65568 | tf_op jit(solution)/shard_map/ppermute | solution.py:140
  135.9 0.6 add_multiply_fusion
  136.7 1.1 copy.14
  (34 shorter events, 1.5 us)
Async XLA Ops:
  0.6 3.7 %copy-start = (bf16[1,256,256]{2,1,0:T(8,128)(2,1)S(1)}, bf16[1,256,256]{2,1,0:T(8,128)(2,1)}, u32[]{:S(2)}) copy-start(bf16[1,256,256]{2,1,0:T(8,128)(2,1)} %param.13) | copy-start | bytes 393220
  4.4 1.6 %copy-start.3 = (f32[4,8,128]{2,1,0:T(8,128)S(1)}, f32[4,8,128]{2,1,0:T(8,128)}, u32[]{:S(2)}) copy-start(f32[4,8,128]{2,1,0:T(8,128)} %param.10) | copy-start | bytes 49156
  4.4 1.7 %copy-start.1 = (f32[64,4,8,128]{3,2,1,0:T(8,128)S(1)}, f32[64,4,8,128]{3,2,1,0:T(8,128)}, u32[]{:S(2)}) copy-start(f32[64,4,8,128]{3,2,1,0:T(8,128)} %param.9) | copy-start | bytes 3145732
  6.2 34.0 %copy-start.5 = (s32[64]{0:T(128)S(1)}, s32[64]{0:T(128)}, u32[]{:S(2)}) copy-start(s32[64]{0:T(128)} %param.17) | copy-start | bytes 772
  40.0 36.9 %copy-start.2 = (f32[256,256]{1,0:T(8,128)S(1)}, f32[256,256]{1,0:T(8,128)}, u32[]{:S(2)}) copy-start(f32[256,256]{1,0:T(8,128)} %param.15) | copy-start | bytes 786436
  40.0 36.9 %copy-start.4 = (s32[256]{0:T(256)S(1)}, s32[256]{0:T(256)}, u32[]{:S(2)}) copy-start(s32[256]{0:T(256)} %param.16) | copy-start | bytes 3076
  40.0 2.0 %collective-permute-start = (f32[64,2,8,128]{3,2,1,0:T(8,128)S(1)}, f32[64,2,8,128]{3,2,1,0:T(8,128)S(1)}, u32[]{:S(2)}, u32[]{:S(2)}) collective-permute-start(f32[64,2,8,128]{3,2,1,0:T(8,128)S(1)} %slice.4), channel_id=1, source_target_pairs={{0,32},{32,0},{64,96},{96,64},{128,160},{160,128},{192,224},{224,1... | collective-permute-start | bytes 1572872 | tf_op jit(solution)/shard_map/ppermute | solution.py:159
  61.4 36.5 %all-to-all-start.1 = ((bf16[256,8,128]{2,1,0:T(8,128)(2,1)}), bf16[256,8,128]{2,1,0:T(8,128)(2,1)S(1)}, u32[]{:S(2)}, u32[]{:S(2)}) async-start(bf16[256,8,128]{2,1,0:T(8,128)(2,1)} %bitcast.7), calls=%async_computation.1 | async-start | bytes 1048576 | tf_op jit(solution)/shard_map/all_to_all | solution.py:172
  98.7 10.6 %collective-permute-start.3 = (f32[64,256]{1,0:T(8,128)S(1)}, f32[64,256]{1,0:T(8,128)S(1)}, u32[]{:S(2)}, u32[]{:S(2)}) collective-permute-start(f32[64,256]{1,0:T(8,128)S(1)} %get-tuple-element.3), channel_id=1, source_target_pairs={{0,3},{1,0},{2,1},{3,2},{4,7},{5,4},{6,5},{7,6},{8,11},{9,8},{10,9... | collective-permute-start | bytes 196616 | tf_op jit(solution)/shard_map/ppermute | solution.py:186
  99.4 9.9 %collective-permute-start.2 = (f32[64,256]{1,0:T(8,128)S(1)}, f32[64,256]{1,0:T(8,128)S(1)}, u32[]{:S(2)}, u32[]{:S(2)}) collective-permute-start(f32[64,256]{1,0:T(8,128)S(1)} %get-tuple-element.4), channel_id=1, source_target_pairs={{0,2},{1,3},{2,0},{3,1},{4,6},{5,7},{6,4},{7,5},{8,10},{9,11},{10,... | collective-permute-start | bytes 196616 | tf_op jit(solution)/shard_map/ppermute | solution.py:186
  102.4 7.3 %collective-permute-start.1 = (f32[64,256]{1,0:T(8,128)S(1)}, f32[64,256]{1,0:T(8,128)S(1)}, u32[]{:S(2)}, u32[]{:S(2)}) collective-permute-start(f32[64,256]{1,0:T(8,128)S(1)} %get-tuple-element.2), channel_id=1, source_target_pairs={{0,1},{1,2},{2,3},{3,0},{4,5},{5,6},{6,7},{7,4},{8,9},{9,10},{10,1... | collective-permute-start | bytes 196616 | tf_op jit(solution)/shard_map/ppermute | solution.py:186
  103.8 32.8 %all-to-all-start.2 = ((bf16[4,64,1024]{2,1,0:T(8,128)(2,1)}), bf16[4,64,1024]{2,1,0:T(8,128)(2,1)S(1)}, u32[]{:S(2)}, u32[]{:S(2)}) async-start(bf16[4,64,1024]{2,1,0:T(8,128)(2,1)} %bitcast.12), calls=%async_computation.2 | async-start | bytes 1048576 | tf_op jit(solution)/shard_map/all_to_all | solution.py:192
  109.7 2.6 %collective-permute-start.4 = (f32[64,256]{1,0:T(8,128)S(1)}, f32[64,256]{1,0:T(8,128)S(1)}, u32[]{:S(2)}, u32[]{:S(2)}) collective-permute-start(f32[64,256]{1,0:T(8,128)S(1)} %fusion.10), channel_id=1, source_target_pairs={{0,32},{32,0},{64,96},{96,64},{128,160},{160,128},{192,224},{224,1... | collective-permute-start | bytes 196616 | tf_op jit(solution)/shard_map/ppermute | solution.py:140
  112.3 8.7 %collective-permute-start.5 = (f32[64,256]{1,0:T(8,128)S(1)}, f32[64,256]{1,0:T(8,128)S(1)}, u32[]{:S(2)}, u32[]{:S(2)}) collective-permute-start(f32[64,256]{1,0:T(8,128)S(1)} %add.87), channel_id=1, source_target_pairs={{0,4},{4,0},{8,12},{12,8},{16,20},{20,16},{24,28},{28,24},{1,5},{5... | collective-permute-start | bytes 196616 | tf_op jit(solution)/shard_map/ppermute | solution.py:140
  121.0 4.5 %collective-permute-start.8 = (f32[64,256]{1,0:T(8,128)S(1)}, f32[64,256]{1,0:T(8,128)S(1)}, u32[]{:S(2)}, u32[]{:S(2)}) collective-permute-start(f32[64,256]{1,0:T(8,128)S(1)} %add.88), channel_id=1, source_target_pairs={{0,192},{32,224},{64,0},{96,32},{128,64},{160,96},{192,128},{224,1... | collective-permute-start | bytes 196616 | tf_op jit(solution)/shard_map/ppermute | solution.py:140
  123.9 4.6 %collective-permute-start.7 = (f32[64,256]{1,0:T(8,128)S(1)}, f32[64,256]{1,0:T(8,128)S(1)}, u32[]{:S(2)}, u32[]{:S(2)}) collective-permute-start(f32[64,256]{1,0:T(8,128)S(1)} %add.88), channel_id=1, source_target_pairs={{0,128},{32,160},{64,192},{96,224},{128,0},{160,32},{192,64},{224,... | collective-permute-start | bytes 196616 | tf_op jit(solution)/shard_map/ppermute | solution.py:140
  124.9 4.3 %collective-permute-start.6 = (f32[64,256]{1,0:T(8,128)S(1)}, f32[64,256]{1,0:T(8,128)S(1)}, u32[]{:S(2)}, u32[]{:S(2)}) collective-permute-start(f32[64,256]{1,0:T(8,128)S(1)} %add.88), channel_id=1, source_target_pairs={{0,64},{32,96},{64,128},{96,160},{128,192},{160,224},{192,0},{224,... | collective-permute-start | bytes 196616 | tf_op jit(solution)/shard_map/ppermute | solution.py:140
  129.3 3.2 %collective-permute-start.11 = (f32[64,256]{1,0:T(8,128)S(1)}, f32[64,256]{1,0:T(8,128)S(1)}, u32[]{:S(2)}, u32[]{:S(2)}) collective-permute-start(f32[64,256]{1,0:T(8,128)S(1)} %add_add_fusion), channel_id=1, source_target_pairs={{0,24},{4,28},{8,0},{12,4},{16,8},{20,12},{24,16},{28,20},{1,25},{... | collective-permute-start | bytes 196616 | tf_op jit(solution)/shard_map/ppermute | solution.py:140
  129.4 4.7 %collective-permute-start.10 = (f32[64,256]{1,0:T(8,128)S(1)}, f32[64,256]{1,0:T(8,128)S(1)}, u32[]{:S(2)}, u32[]{:S(2)}) collective-permute-start(f32[64,256]{1,0:T(8,128)S(1)} %add_add_fusion), channel_id=1, source_target_pairs={{0,16},{4,20},{8,24},{12,28},{16,0},{20,4},{24,8},{28,12},{1,17},{... | collective-permute-start | bytes 196616 | tf_op jit(solution)/shard_map/ppermute | solution.py:140
  131.6 4.3 %collective-permute-start.9 = (f32[64,256]{1,0:T(8,128)S(1)}, f32[64,256]{1,0:T(8,128)S(1)}, u32[]{:S(2)}, u32[]{:S(2)}) collective-permute-start(f32[64,256]{1,0:T(8,128)S(1)} %add_add_fusion), channel_id=1, source_target_pairs={{0,8},{4,12},{8,16},{12,20},{16,24},{20,28},{24,0},{28,4},{1,9},{5... | collective-permute-start | bytes 196616 | tf_op jit(solution)/shard_map/ppermute | solution.py:140

commit v2 on v1

--- a/solution.py
+++ b/solution.py
@@ -35,12 +35,21 @@
     hidden = jax.nn.silu(jnp.dot(w_hidden[0], hidden, preferred_element_type=jnp.float32)).astype(
         jnp.bfloat16
     )
-    values = jnp.tanh(jnp.dot(w_last[None, :], hidden, preferred_element_type=jnp.float32)[0])
+    values = jnp.tanh(
+        jnp.dot(
+            jnp.broadcast_to(w_last, (8, w_last.shape[0])),
+            hidden,
+            preferred_element_type=jnp.float32,
+        )[0]
+    )
     return values.reshape(cell_features.shape[1:])
 
 
 NX, NY, NZ = 32, 64, 128
 PAD = 8
+TOGETHER = 16
+ORBITAL_SCALE = 8192.0
+POTENTIAL_MIDDLE = 1.0
 
 
 def filter_kernel(info, taken, other, out, field, shifted):
@@ -53,62 +62,66 @@
         field[which, 0] = edge
         field[which, NX + 1] = edge
 
-    def load(plane, carry):
-        outer = lax.div(plane, 4)
-        inner = lax.rem(plane, 4)
-        half = lax.div(inner, 2)
-        place = lax.rem(inner, 2)
-        for which in range(2):
-            field[which, plane + 1, 0:PAD] = rim
-            field[which, plane + 1, PAD + NY :] = rim
-        for run in range(8):
-            rows = slice(PAD + 8 * run, PAD + 8 * run + 8)
-            block = taken[outer * 8 + run, inner]
-            field[0, plane + 1, rows] = block
-            field[1, plane + 1, rows] = block
-            own = taken[outer * 8 + run, 4 + place]
-            far = other[outer * 8 + run, place]
-            value = jnp.where(half == core, own, far)
-            shifted[plane, 8 * run : 8 * run + 8] = value + (3.0 - centre)
+    def load(outer, carry):
+        for inner in range(4):
+            plane = outer * 4 + inner
+            for which in range(2):
+                field[which, plane + 1, 0:PAD] = rim
+                field[which, plane + 1, PAD + NY :] = rim
+            for run in range(8):
+                rows = slice(PAD + 8 * run, PAD + 8 * run + 8)
+                field[0, plane + 1, rows] = taken[outer * 8 + run, inner] * (1.0 / ORBITAL_SCALE)
+                own = taken[outer * 8 + run, 4 + inner % 2]
+                far = other[outer * 8 + run, inner % 2]
+                value = jnp.where(inner // 2 == core, own, far)
+                shifted[plane, 8 * run : 8 * run + 8] = value + (POTENTIAL_MIDDLE + 3.0 - centre)
         return carry
 
-    lax.fori_loop(0, NX, load, 0)
-    lane = lax.broadcasted_iota(jnp.int32, (NY, NZ), 1)
+    lax.fori_loop(0, NX // 4, load, 0)
+    lane = lax.broadcasted_iota(jnp.int32, (8, NZ), 1)
     not_first = lane > 0
     not_last = lane < NZ - 1
+
+    def tile(now, then, x, row, scale_new, scale_old):
+        low = PAD + row
+        here = field[now, x, low : low + 8]
+        beside = field[now, x - 1, low : low + 8] + field[now, x + 1, low : low + 8]
+        beside += field[now, x, low - 1 : low + 7] + field[now, x, low + 1 : low + 9]
+        beside += jnp.where(not_first, pltpu.roll(here, 1, 1), 0.0) + jnp.where(
+            not_last, pltpu.roll(here, NZ - 1, 1), 0.0
+        )
+        fresh = (scale_new * shifted[x - 1, row : row + 8]) * here - (0.5 * scale_new) * beside
+        if scale_old != 0.0:
+            fresh -= scale_old * field[then, x, low : low + 8]
+        field[then, x, low : low + 8] = fresh
+
     for rounds in range(DEG):
         scale_new, scale_old = factors[rounds]
         now = rounds % 2
-        then = 1 - now
 
         @pl.when(rounds < degree)
         def _():
-            def step(plane, carry):
-                x = plane + 1
-                here = field[now, x, PAD : PAD + NY]
-                beside = field[now, x - 1, PAD : PAD + NY] + field[now, x + 1, PAD : PAD + NY]
-                beside += (
-                    field[now, x, PAD - 1 : PAD + NY - 1] + field[now, x, PAD + 1 : PAD + NY + 1]
-                )
-                beside += jnp.where(not_first, pltpu.roll(here, 1, 1), 0.0)
-                beside += jnp.where(not_last, pltpu.roll(here, NZ - 1, 1), 0.0)
-                fresh = scale_new * (shifted[plane] * here - 0.5 * beside)
-                if scale_old != 0.0:
-                    fresh -= scale_old * field[then, x, PAD : PAD + NY]
-                field[then, x, PAD : PAD + NY] = fresh
+            def step(turn, carry):
+                for part in range(TOGETHER):
+                    for row in range(0, NY, 8):
+                        tile(now, 1 - now, turn * TOGETHER + part + 1, row, scale_new, scale_old)
                 return carry
 
-            lax.fori_loop(0, NX, step, 0)
+            lax.fori_loop(0, NX // TOGETHER, step, 0)
 
     last = lax.rem(degree, 2)
 
-    def store(plane, carry):
-        out[lax.rem(plane, 4), lax.div(plane, 4)] = field[last, plane + 1, PAD : PAD + NY].astype(
-            jnp.bfloat16
-        )
+    def store(outer, carry):
+        for inner in range(4):
+            out[inner, outer] = field[last, outer * 4 + inner + 1, PAD : PAD + NY].astype(
+                jnp.bfloat16
+            )
         return carry
 
-    lax.fori_loop(0, NX, store, 0)
+    lax.fori_loop(0, NX // 4, store, 0)
+
+
+ACROSS = [(i, i ^ 1) for i in range(8)]
 
 
 def run_filter(info, taken, other):
@@ -154,12 +167,14 @@
     potential = v_local + network(features, w_first, w_hidden, w_last)
     halves = potential.reshape(1, 2, 1, 2, size_y, size_z)
     halves = jnp.broadcast_to(halves, (4, 2, 8, 2, size_y, size_z)).reshape(64, 2, size_y, size_z)
-    message = jnp.concatenate([orbitals, halves], axis=1)
+    message = jnp.concatenate([orbitals * ORBITAL_SCALE, halves - POTENTIAL_MIDDLE], axis=1)
+    message = message.astype(jnp.float16)
+    core = lax.rem(gx, 2)
+    degree = lax.dynamic_index_in_dim(degrees, gx * 8 + gyz, 0, keepdims=False)
+    info = jnp.stack([core, degree]).astype(jnp.int32)
     taken = lax.all_to_all(message, ("gx", "gyz"), 0, 0, tiled=True)
-    other = lax.ppermute(taken[:, 4:], "gx", [(i, i ^ 1) for i in range(8)])
-    degree = lax.dynamic_index_in_dim(degrees, gx * 8 + gyz, 0, keepdims=False)
-    info = jnp.stack([lax.rem(gx, 2), degree]).astype(jnp.int32)
-    filtered = run_filter(info, taken, other)
+    other = lax.ppermute(taken[:, 4:], "gx", ACROSS)
+    filtered = run_filter(info, taken.astype(jnp.float32), other.astype(jnp.float32))
 
     select = (assignment[:, None] == lax.iota(jnp.int32, total_slots)[None, :]).astype(jnp.bfloat16)
     permuted = jnp.dot(
@@ -171,27 +186,39 @@
 
     panel = lax.all_to_all(
         filtered.reshape(256, 8, 128), ("band", "gx", "gyz"), 0, 0, tiled=True
-    ).reshape(256, 1024)
+    )
+    panel, slot_rotation = lax.optimization_barrier((panel, slot_rotation))
+    panel = panel.reshape(256, 1024)
     margin = lax.dot_general(
         panel, panel, (((1,), (1,)), ((), ())), preferred_element_type=jnp.float32
     )
+    half = total_slots // 2
+    kept = jnp.where(core == 0, margin[:, :half], margin[:, half:])
+    sent = jnp.where(core == 0, margin[:, half:], margin[:, :half])
+    rows = (kept + lax.ppermute(sent, "gx", ACROSS)).reshape(4, local_slots, half)
+    rows, panel = lax.optimization_barrier((rows, panel))
     turned = lax.dot_general(
         slot_rotation, panel, (((0,), (0,)), ((), ())), preferred_element_type=jnp.float32
     ).astype(jnp.bfloat16)
-
-    rows = margin.reshape(4, local_slots, total_slots)
     gram = lax.dynamic_index_in_dim(rows, band, 0, keepdims=False)
     for shift in range(1, 4):
         piece = lax.dynamic_index_in_dim(rows, lax.rem(band + shift, 4), 0, keepdims=False)
         gram = gram + lax.ppermute(piece, "band", [(i, (i + shift) % 4) for i in range(4)])
-    gram = reduce_over(gram, "gx", 1, 2)
+    gram = reduce_over(gram, "gx", 2, 4)
+    gram = reduce_over(gram, "gyz", 2, 4)
+    back = lax.all_to_all(turned.reshape(4, local_slots, 1024), "band", 0, 0, tiled=True)
     gram = reduce_over(gram, "gyz", 1, 2)
-    gram = reduce_over(gram, "gx", 2, 4)
-    gram = reduce_over(gram, "gyz", 2, 4) / total_cells
-
-    back = lax.all_to_all(turned.reshape(4, local_slots, 1024), "band", 0, 0, tiled=True)
+    gram, back = lax.optimization_barrier((gram, back))
     rotated = jnp.swapaxes(back, 0, 1).reshape(local_slots, size_x, size_y, size_z)
-    return (gram, rotated.astype(jnp.float32))
+    rotated = rotated.astype(jnp.float32)
+    beyond = lax.ppermute(gram, "gx", ACROSS)
+    gram = (
+        jnp.concatenate(
+            [jnp.where(core == 0, gram, beyond), jnp.where(core == 0, beyond, gram)], axis=1
+        )
+        / total_cells
+    )
+    return (gram, rotated)
 
 
 def solution(mesh):

time: 140 us -> 106 us (0.76); the launches traced: 138 us -> 106 us
  Pallas kernels: 19.4 us -> 4.38 us
  blocking collectives: 33.7 us -> 25.5 us
  waiting for transfers between devices: 37.3 us -> 29.7 us
    pallas_call x1, Pallas kernels: 19.4 us -> 4.38 us  [run_filter(): pl.pallas_call(filter_kernel, out_shape=jax.ShapeDtypeStruct((4, 8, NY, N...]
    all_to_all x1, blocking collectives: 33.7 us -> 25.5 us  [on_device(): taken = lax.all_to_all(message, ('gx', 'gyz'), 0, 0, tiled=True)]
    ppermute x8 -> x7, waiting for transfers between devices: 15.7 us -> 8.05 us  [reduce_over(): total = total + lax.ppermute(value, axis, pairs)]
    ppermute x1 -> x3, starting transfers between devices: 0.23 us -> 6.39 us  [the longest x1 5.27 us: on_device(): beyond = lax.ppermute(gram, 'gx', ACROSS)]
    ppermute x8 -> x7, starting transfers between devices: 10.5 us -> 6.17 us  [reduce_over(): total = total + lax.ppermute(value, axis, pairs)]
    all_to_all x1, starting transfers between devices: 15.4 us -> 12.1 us  [on_device(): lax.all_to_all(filtered.reshape(256, 8, 128), ('band', 'gx', 'gyz'), 0, 0...]
  transfers between devices with their start and end apart: 14 -> 15, of which waited for: 10 -> 9; matrix products, arithmetic and copies ran while one was open for 3% -> 4% of each run, Pallas kernels for 0% -> 0%
where the time goes in v2:
time: 106 us
  starting transfers between devices  34.9 us (33%)
  waiting for transfers between devices  29.7 us (28%)
  blocking collectives  25.5 us (24%)
  matrix products  5.53 us (5%)
  Pallas kernels  4.38 us (4%)
  local copies, waits for them, and re-layouts  3.31 us (3%)
  other arithmetic  1.93 us (2%)
    all_to_all x1, blocking collectives, on_device(): taken = lax.all_to_all(message, ('gx', 'gyz'), 0, 0, tiled=True)  25.5 us
    all_to_all x1, waiting for transfers between devices, on_device(): lax.all_to_all(filtered.reshape(256, 8, 128), ('band', 'gx', 'gyz'), 0, 0...  20.7 us
    all_to_all x1, starting transfers between devices, on_device(): lax.all_to_all(filtered.reshape(256, 8, 128), ('band', 'gx', 'gyz'), 0, 0...  12.1 us
    ppermute x7, waiting for transfers between devices, reduce_over(): total = total + lax.ppermute(value, axis, pairs)  8.05 us
    all_to_all x1, starting transfers between devices, on_device(): lax.all_to_all(turned.reshape(4, local_slots, 1024), 'band', 0, 0, tiled=...  6.21 us
    ppermute x7, starting transfers between devices, reduce_over(): total = total + lax.ppermute(value, axis, pairs)  6.17 us
    ppermute x1, starting transfers between devices, on_device(): beyond = lax.ppermute(gram, 'gx', ACROSS)  5.27 us
    pallas_call x1, Pallas kernels, run_filter(): pl.pallas_call(filter_kernel, out_shape=jax.ShapeDtypeStruct((4, 8, NY, N...  4.38 us
  transfers between devices with their start and end apart: 15, of which 9 were waited for; matrix products, arithmetic and copies ran while one was open for 4% of the time, Pallas kernels for 0%

profile of v2, /device:TPU:1, one launch (start us, length us, event | category | flops | bytes accessed | tf_op | source)
XLA Modules:
  0.0 106.2 jit_solution(15246292341101542522)
XLA Ops:
  0.6 0.9 pad.6
  1.7 2.1 %multiply_convert_fusion.1 = bf16[256,4096]{1,0:T(8,128)(2,1)S(1)} fusion(bf16[256,11]{0,1:T(8,128)(2,1)} %param.12, bf16[11,4096]{1,0:T(8,128)(2,1)S(1)} %bitcast.60), kind=kOutput, calls=%fused_computation.3 | convolution fusion | flops 28311552 | bytes 2192896 | tf_op jit(solution)/shard_map/dot_general | solution.py:32
  3.8 1.6 %convolution_bitcast_fusion.1 = f32[8,4096]{1,0:T(8,128)S(1)} fusion(bf16[256,4096]{1,0:T(8,128)(2,1)S(1)} %multiply_convert_fusion.1, bf16[1,256,256]{2,1,0:T(8,128)(2,1)S(1)} %copy-done, bf16[256]{0:T(256)(128)(2,1)S(1)} %copy-done.5), kind=kOutput, calls=%fused_computation.1 | convolution fusion | flops 558891008 | bytes 2359808 | tf_op jit(solution)/shard_map/dot_general | solution.py:39
  5.9 25.5 %all_to_all.15 = f16[64,6,8,128]{3,2,1,0:T(8,128)(2,1)S(1)} all-to-all(f16[64,6,8,128]{3,2,1,0:T(8,128)(2,1)S(1)} %pad_maximum_fusion), channel_id=1, replica_groups=mesh['gx'=8,'gyz'=8,'band'=4] {'gx','gyz'}, dimensions={0} | all-to-all | bytes 1572864 | tf_op jit(solution)/shard_map/all_to_all | solution.py:175
  31.7 0.6 dynamic_slice.17
  32.3 0.7 pad_add_fusion.info
  33.2 4.4 %shard_map.104 = bf16[4,8,64,128]{3,2,1,0:T(8,128)(2,1)} custom-call(s32[2]{0:T(128)S(1)} %pad_add_fusion.info, f32[64,6,8,128]{3,2,1,0:T(8,128)S(1)} %convert_element_type.37.taken, f32[64,2,8,128]{3,2,1,0:T(8,128)S(1)} %convert_element_type.38.other), custom_call_target="tpu_custom_call" | custom-call | flops 33554432 | bytes 3145728 | tf_op jit(solution)/shard_map/pallas_call | solution.py:129
  37.6 12.1 %all-to-all-start.1 = ((bf16[256,8,128]{2,1,0:T(8,128)(2,1)}), bf16[256,8,128]{2,1,0:T(8,128)(2,1)S(1)}, u32[]{:S(2)}, u32[]{:S(2)}) async-start(bf16[256,8,128]{2,1,0:T(8,128)(2,1)} %bitcast.7), calls=%async_computation.1 | async-start | bytes 1048576 | tf_op jit(solution)/shard_map/all_to_all | solution.py:187
  50.1 20.7 %all-to-all-done.1 = bf16[256,8,128]{2,1,0:T(8,128)(2,1)S(1)} async-done(((bf16[256,8,128]{2,1,0:T(8,128)(2,1)}), bf16[256,8,128]{2,1,0:T(8,128)(2,1)S(1)}, u32[]{:S(2)}, u32[]{:S(2)}) %all-to-all-start.1) | async-done | bytes 524320 | tf_op jit(solution)/shard_map/all_to_all | solution.py:187
  71.4 0.8 collective-permute-start.1
  72.3 1.0 collective-permute-done.1
  73.3 0.6 collective-permute-start.2
  73.9 1.8 %collective-permute-start.3 = (f32[64,128]{1,0:T(8,128)S(1)}, f32[64,128]{1,0:T(8,128)S(1)}, u32[]{:S(2)}, u32[]{:S(2)}) collective-permute-start(f32[64,128]{1,0:T(8,128)S(1)} %get-tuple-element.16), channel_id=1, source_target_pairs={{0,2},{1,3},{2,0},{3,1},{4,6},{5,7},{6,4},{7,5},{8,10},{9,11},{10,... | collective-permute-start | bytes 98312 | tf_op jit(solution)/shard_map/ppermute | solution.py:206
  75.7 1.7 %collective-permute-start.4 = (f32[64,128]{1,0:T(8,128)S(1)}, f32[64,128]{1,0:T(8,128)S(1)}, u32[]{:S(2)}, u32[]{:S(2)}) collective-permute-start(f32[64,128]{1,0:T(8,128)S(1)} %get-tuple-element.15), channel_id=1, source_target_pairs={{0,3},{1,0},{2,1},{3,2},{4,7},{5,4},{6,5},{7,6},{8,11},{9,8},{10,9... | collective-permute-start | bytes 98312 | tf_op jit(solution)/shard_map/ppermute | solution.py:206
  77.4 1.1 %convolution_convert_fusion = bf16[256,1024]{1,0:T(8,128)(2,1)} fusion(bf16[256,256]{1,0:T(8,128)(2,1)S(1)} %convolution_convert_fusion.1, bf16[256,1024]{0,1:T(8,128)(2,1)S(1)} %bitcast.53), kind=kOutput, calls=%fused_computation.4 | convolution fusion | flops 134479872 | bytes 1179648 | tf_op jit(solution)/shard_map/dot_general | solution.py:200
  78.5 6.2 %all-to-all-start.2 = ((bf16[4,64,1024]{2,1,0:T(8,128)(2,1)}), bf16[4,64,1024]{2,1,0:T(8,128)(2,1)S(1)}, u32[]{:S(2)}, u32[]{:S(2)}) async-start(bf16[4,64,1024]{2,1,0:T(8,128)(2,1)} %bitcast.15), calls=%async_computation.2 | async-start | bytes 1048576 | tf_op jit(solution)/shard_map/all_to_all | solution.py:209
  84.9 1.8 %collective-permute-start.6 = (f32[64,128]{1,0:T(8,128)S(1)}, f32[64,128]{1,0:T(8,128)S(1)}, u32[]{:S(2)}, u32[]{:S(2)}) collective-permute-start(f32[64,128]{1,0:T(8,128)S(1)} %fusion.7), channel_id=1, source_target_pairs={{0,128},{32,160},{64,192},{96,224},{128,0},{160,32},{192,64},{224,... | collective-permute-start | bytes 98312 | tf_op jit(solution)/shard_map/ppermute | solution.py:153
  86.7 1.2 %collective-permute-start.7 = (f32[64,128]{1,0:T(8,128)S(1)}, f32[64,128]{1,0:T(8,128)S(1)}, u32[]{:S(2)}, u32[]{:S(2)}) collective-permute-start(f32[64,128]{1,0:T(8,128)S(1)} %fusion.7), channel_id=1, source_target_pairs={{0,192},{32,224},{64,0},{96,32},{128,64},{160,96},{192,128},{224,1... | collective-permute-start | bytes 98312 | tf_op jit(solution)/shard_map/ppermute | solution.py:153
  87.9 1.0 collective-permute-done.5
  88.8 0.4 collective-permute-done.6
  89.2 0.5 collective-permute-done.7
  89.8 0.6 collective-permute-start.10
  90.3 1.0 collective-permute-start.8
  91.3 0.7 collective-permute-start.9
  92.0 0.9 collective-permute-done.10
  92.9 1.7 %collective-permute-done.8 = f32[64,128]{1,0:T(8,128)S(1)} collective-permute-done((f32[64,128]{1,0:T(8,128)S(1)}, f32[64,128]{1,0:T(8,128)S(1)}, u32[]{:S(2)}, u32[]{:S(2)}) %collective-permute-start.8) | collective-permute-done | bytes 32800 | tf_op jit(solution)/shard_map/ppermute | solution.py:153
  94.6 1.3 %collective-permute-done.9 = f32[64,128]{1,0:T(8,128)S(1)} collective-permute-done((f32[64,128]{1,0:T(8,128)S(1)}, f32[64,128]{1,0:T(8,128)S(1)}, u32[]{:S(2)}, u32[]{:S(2)}) %collective-permute-start.9) | collective-permute-done | bytes 32800 | tf_op jit(solution)/shard_map/ppermute | solution.py:153
  95.9 0.9 collective-permute-start.11
  96.8 2.3 %collective-permute-done.11 = f32[64,128]{1,0:T(8,128)S(1)} collective-permute-done((f32[64,128]{1,0:T(8,128)S(1)}, f32[64,128]{1,0:T(8,128)S(1)}, u32[]{:S(2)}, u32[]{:S(2)}) %collective-permute-start.11) | collective-permute-done | bytes 32800 | tf_op jit(solution)/shard_map/ppermute | solution.py:153
  99.1 5.3 %collective-permute-start.12 = (f32[64,128]{1,0:T(8,128)S(1)}, f32[64,128]{1,0:T(8,128)S(1)}, u32[]{:S(2)}, u32[]{:S(2)}) collective-permute-start(f32[64,128]{1,0:T(8,128)S(1)} %add.98), channel_id=1, source_target_pairs={{0,32},{32,0},{64,96},{96,64},{128,160},{160,128},{192,224},{224,1... | collective-permute-start | bytes 98312 | tf_op jit(solution)/shard_map/ppermute | solution.py:214
  104.4 1.1 %copy.25 = f32[64,4,8,128]{3,2,1,0:T(8,128)} copy(f32[64,4,8,128]{3,2,0,1:T(8,128)S(1)} %bitcast.54) | data formatting | bytes 2097152 | tf_op jit(solution)/shard_map/convert_element_type | solution.py:213
  105.6 0.6 maximum_multiply_fusion
  (43 shorter events, 2.4 us)
Async XLA Ops:
  0.6 3.1 %copy-start = (bf16[1,256,256]{2,1,0:T(8,128)(2,1)S(1)}, bf16[1,256,256]{2,1,0:T(8,128)(2,1)}, u32[]{:S(2)}) copy-start(bf16[1,256,256]{2,1,0:T(8,128)(2,1)} %param.13) | copy-start | bytes 393220
  1.6 2.1 %copy-start.5 = (bf16[256]{0:T(256)(128)(2,1)S(1)}, bf16[256]{0:T(256)(128)(2,1)}, u32[]{:S(2)}) copy-start(bf16[256]{0:T(256)(128)(2,1)} %param.14) | copy-start | bytes 1540
  3.8 1.7 %copy-start.1 = (f32[64,4,8,128]{3,2,1,0:T(8,128)S(1)}, f32[64,4,8,128]{3,2,1,0:T(8,128)}, u32[]{:S(2)}) copy-start(f32[64,4,8,128]{3,2,1,0:T(8,128)} %param.9) | copy-start | bytes 3145732
  3.8 1.8 %copy-start.3 = (f32[4,8,128]{2,1,0:T(8,128)S(1)}, f32[4,8,128]{2,1,0:T(8,128)}, u32[]{:S(2)}) copy-start(f32[4,8,128]{2,1,0:T(8,128)} %param.10) | copy-start | bytes 49156
  5.6 26.1 %copy-start.6 = (s32[64]{0:T(128)S(1)}, s32[64]{0:T(128)}, u32[]{:S(2)}) copy-start(s32[64]{0:T(128)} %param.17) | copy-start | bytes 772
  31.4 1.8 %collective-permute-start = (f16[64,2,8,128]{3,2,1,0:T(8,128)(2,1)S(1)}, f16[64,2,8,128]{3,2,1,0:T(8,128)(2,1)S(1)}, u32[]{:S(2)}, u32[]{:S(2)}) collective-permute-start(f16[64,2,8,128]{3,2,1,0:T(8,128)(2,1)S(1)} %slice.19), channel_id=1, source_target_pairs={{0,32},{32,0},{64,96},{96,64},{128,160},{160,128},{192,224},{224,1... | collective-permute-start | bytes 786440 | tf_op jit(solution)/shard_map/ppermute | solution.py:176
  33.1 16.6 %copy-start.2 = (f32[256,256]{1,0:T(8,128)S(1)}, f32[256,256]{1,0:T(8,128)}, u32[]{:S(2)}) copy-start(f32[256,256]{1,0:T(8,128)} %param.15) | copy-start | bytes 786436
  33.1 16.6 %copy-start.4 = (s32[256]{0:T(256)S(1)}, s32[256]{0:T(256)}, u32[]{:S(2)}) copy-start(s32[256]{0:T(256)} %param.16) | copy-start | bytes 3076
  37.6 33.2 %all-to-all-start.1 = ((bf16[256,8,128]{2,1,0:T(8,128)(2,1)}), bf16[256,8,128]{2,1,0:T(8,128)(2,1)S(1)}, u32[]{:S(2)}, u32[]{:S(2)}) async-start(bf16[256,8,128]{2,1,0:T(8,128)(2,1)} %bitcast.7), calls=%async_computation.1 | async-start | bytes 1048576 | tf_op jit(solution)/shard_map/all_to_all | solution.py:187
  71.4 1.8 %collective-permute-start.1 = (f32[256,128]{1,0:T(8,128)S(1)}, f32[256,128]{1,0:T(8,128)S(1)}, u32[]{:S(2)}, u32[]{:S(2)}) collective-permute-start(f32[256,128]{1,0:T(8,128)S(1)} %slice_select_fusion), channel_id=1, source_target_pairs={{0,32},{32,0},{64,96},{96,64},{128,160},{160,128},{192,224},{224,1... | collective-permute-start | bytes 393224 | tf_op jit(solution)/shard_map/ppermute | solution.py:198
  73.3 11.4 %collective-permute-start.2 = (f32[64,128]{1,0:T(8,128)S(1)}, f32[64,128]{1,0:T(8,128)S(1)}, u32[]{:S(2)}, u32[]{:S(2)}) collective-permute-start(f32[64,128]{1,0:T(8,128)S(1)} %get-tuple-element.14), channel_id=1, source_target_pairs={{0,1},{1,2},{2,3},{3,0},{4,5},{5,6},{6,7},{7,4},{8,9},{9,10},{10,1... | collective-permute-start | bytes 98312 | tf_op jit(solution)/shard_map/ppermute | solution.py:206
  73.9 10.8 %collective-permute-start.3 = (f32[64,128]{1,0:T(8,128)S(1)}, f32[64,128]{1,0:T(8,128)S(1)}, u32[]{:S(2)}, u32[]{:S(2)}) collective-permute-start(f32[64,128]{1,0:T(8,128)S(1)} %get-tuple-element.16), channel_id=1, source_target_pairs={{0,2},{1,3},{2,0},{3,1},{4,6},{5,7},{6,4},{7,5},{8,10},{9,11},{10,... | collective-permute-start | bytes 98312 | tf_op jit(solution)/shard_map/ppermute | solution.py:206
  75.7 9.0 %collective-permute-start.4 = (f32[64,128]{1,0:T(8,128)S(1)}, f32[64,128]{1,0:T(8,128)S(1)}, u32[]{:S(2)}, u32[]{:S(2)}) collective-permute-start(f32[64,128]{1,0:T(8,128)S(1)} %get-tuple-element.15), channel_id=1, source_target_pairs={{0,3},{1,0},{2,1},{3,2},{4,7},{5,4},{6,5},{7,6},{8,11},{9,8},{10,9... | collective-permute-start | bytes 98312 | tf_op jit(solution)/shard_map/ppermute | solution.py:206
  78.5 20.5 %all-to-all-start.2 = ((bf16[4,64,1024]{2,1,0:T(8,128)(2,1)}), bf16[4,64,1024]{2,1,0:T(8,128)(2,1)S(1)}, u32[]{:S(2)}, u32[]{:S(2)}) async-start(bf16[4,64,1024]{2,1,0:T(8,128)(2,1)} %bitcast.15), calls=%async_computation.2 | async-start | bytes 1048576 | tf_op jit(solution)/shard_map/all_to_all | solution.py:209
  84.8 4.1 %collective-permute-start.5 = (f32[64,128]{1,0:T(8,128)S(1)}, f32[64,128]{1,0:T(8,128)S(1)}, u32[]{:S(2)}, u32[]{:S(2)}) collective-permute-start(f32[64,128]{1,0:T(8,128)S(1)} %fusion.7), channel_id=1, source_target_pairs={{0,64},{32,96},{64,128},{96,160},{128,192},{160,224},{192,0},{224,... | collective-permute-start | bytes 98312 | tf_op jit(solution)/shard_map/ppermute | solution.py:153
  84.9 4.4 %collective-permute-start.6 = (f32[64,128]{1,0:T(8,128)S(1)}, f32[64,128]{1,0:T(8,128)S(1)}, u32[]{:S(2)}, u32[]{:S(2)}) collective-permute-start(f32[64,128]{1,0:T(8,128)S(1)} %fusion.7), channel_id=1, source_target_pairs={{0,128},{32,160},{64,192},{96,224},{128,0},{160,32},{192,64},{224,... | collective-permute-start | bytes 98312 | tf_op jit(solution)/shard_map/ppermute | solution.py:153
  86.7 3.1 %collective-permute-start.7 = (f32[64,128]{1,0:T(8,128)S(1)}, f32[64,128]{1,0:T(8,128)S(1)}, u32[]{:S(2)}, u32[]{:S(2)}) collective-permute-start(f32[64,128]{1,0:T(8,128)S(1)} %fusion.7), channel_id=1, source_target_pairs={{0,192},{32,224},{64,0},{96,32},{128,64},{160,96},{192,128},{224,1... | collective-permute-start | bytes 98312 | tf_op jit(solution)/shard_map/ppermute | solution.py:153
  89.8 3.1 %collective-permute-start.10 = (f32[64,128]{1,0:T(8,128)S(1)}, f32[64,128]{1,0:T(8,128)S(1)}, u32[]{:S(2)}, u32[]{:S(2)}) collective-permute-start(f32[64,128]{1,0:T(8,128)S(1)} %add_add_fusion.1), channel_id=1, source_target_pairs={{0,24},{4,28},{8,0},{12,4},{16,8},{20,12},{24,16},{28,20},{1,25},{... | collective-permute-start | bytes 98312 | tf_op jit(solution)/shard_map/ppermute | solution.py:153
  90.3 4.3 %collective-permute-start.8 = (f32[64,128]{1,0:T(8,128)S(1)}, f32[64,128]{1,0:T(8,128)S(1)}, u32[]{:S(2)}, u32[]{:S(2)}) collective-permute-start(f32[64,128]{1,0:T(8,128)S(1)} %add_add_fusion.1), channel_id=1, source_target_pairs={{0,8},{4,12},{8,16},{12,20},{16,24},{20,28},{24,0},{28,4},{1,9},{5... | collective-permute-start | bytes 98312 | tf_op jit(solution)/shard_map/ppermute | solution.py:153
  91.3 4.6 %collective-permute-start.9 = (f32[64,128]{1,0:T(8,128)S(1)}, f32[64,128]{1,0:T(8,128)S(1)}, u32[]{:S(2)}, u32[]{:S(2)}) collective-permute-start(f32[64,128]{1,0:T(8,128)S(1)} %add_add_fusion.1), channel_id=1, source_target_pairs={{0,16},{4,20},{8,24},{12,28},{16,0},{20,4},{24,8},{28,12},{1,17},{... | collective-permute-start | bytes 98312 | tf_op jit(solution)/shard_map/ppermute | solution.py:153
  95.9 3.1 %collective-permute-start.11 = (f32[64,128]{1,0:T(8,128)S(1)}, f32[64,128]{1,0:T(8,128)S(1)}, u32[]{:S(2)}, u32[]{:S(2)}) collective-permute-start(f32[64,128]{1,0:T(8,128)S(1)} %add_add_fusion), channel_id=1, source_target_pairs={{0,4},{4,0},{8,12},{12,8},{16,20},{20,16},{24,28},{28,24},{1,5},{5... | collective-permute-start | bytes 98312 | tf_op jit(solution)/shard_map/ppermute | solution.py:153
  99.1 6.5 %collective-permute-start.12 = (f32[64,128]{1,0:T(8,128)S(1)}, f32[64,128]{1,0:T(8,128)S(1)}, u32[]{:S(2)}, u32[]{:S(2)}) collective-permute-start(f32[64,128]{1,0:T(8,128)S(1)} %add.98), channel_id=1, source_target_pairs={{0,32},{32,0},{64,96},{96,64},{128,160},{160,128},{192,224},{224,1... | collective-permute-start | bytes 98312 | tf_op jit(solution)/shard_map/ppermute | solution.py:214

commit v3 on v2

--- a/solution.py
+++ b/solution.py
@@ -26,15 +26,16 @@
     return (factors, centre)
 
 
+def silu(value):
+    half = 0.5 * value
+    return (half + half * jnp.tanh(half)).astype(jnp.bfloat16)
+
+
 def network(cell_features, w_first, w_hidden, w_last):
     feature_count = cell_features.shape[0]
     flattened = cell_features.reshape(feature_count, -1)
-    hidden = jax.nn.silu(jnp.dot(w_first, flattened, preferred_element_type=jnp.float32)).astype(
-        jnp.bfloat16
-    )
-    hidden = jax.nn.silu(jnp.dot(w_hidden[0], hidden, preferred_element_type=jnp.float32)).astype(
-        jnp.bfloat16
-    )
+    hidden = silu(jnp.dot(w_first, flattened, preferred_element_type=jnp.float32))
+    hidden = silu(jnp.dot(w_hidden[0], hidden, preferred_element_type=jnp.float32))
     values = jnp.tanh(
         jnp.dot(
             jnp.broadcast_to(w_last, (8, w_last.shape[0])),
@@ -47,7 +48,7 @@
 
 NX, NY, NZ = 32, 64, 128
 PAD = 8
-TOGETHER = 16
+TOGETHER = 32
 ORBITAL_SCALE = 8192.0
 POTENTIAL_MIDDLE = 1.0
 
@@ -145,13 +146,18 @@
 def reduce_over(value, axis, step, count):
     size = lax.axis_size(axis)
     total = value
+    sent = value.astype(jnp.bfloat16)
     for shift in range(1, count):
         pairs = []
         for i in range(size):
             place = (i // step) % count
             pairs.append((i, i + (((place + shift) % count) - place) * step))
-        total = total + lax.ppermute(value, axis, pairs)
+        total = total + lax.ppermute(sent, axis, pairs).astype(value.dtype)
     return total
+
+
+def to_band(value, shift):
+    return lax.ppermute(value, "band", [(i, (i + shift) % 4) for i in range(4)])
 
 
 def on_device(
@@ -191,33 +197,37 @@
     panel = panel.reshape(256, 1024)
     margin = lax.dot_general(
         panel, panel, (((1,), (1,)), ((), ())), preferred_element_type=jnp.float32
-    )
-    half = total_slots // 2
-    kept = jnp.where(core == 0, margin[:, :half], margin[:, half:])
-    sent = jnp.where(core == 0, margin[:, half:], margin[:, :half])
-    rows = (kept + lax.ppermute(sent, "gx", ACROSS)).reshape(4, local_slots, half)
-    rows, panel = lax.optimization_barrier((rows, panel))
+    ) * (1.0 / total_cells)
+    rows = margin.reshape(4, local_slots, total_slots)
+    gram = lax.dynamic_index_in_dim(rows, band, 0, keepdims=False)
+    for shift in range(1, 4):
+        piece = lax.dynamic_index_in_dim(rows, lax.rem(band + shift, 4), 0, keepdims=False)
+        gram = gram + to_band(piece.astype(jnp.bfloat16), shift).astype(jnp.float32)
+
     turned = lax.dot_general(
         slot_rotation, panel, (((0,), (0,)), ((), ())), preferred_element_type=jnp.float32
     ).astype(jnp.bfloat16)
-    gram = lax.dynamic_index_in_dim(rows, band, 0, keepdims=False)
-    for shift in range(1, 4):
-        piece = lax.dynamic_index_in_dim(rows, lax.rem(band + shift, 4), 0, keepdims=False)
-        gram = gram + lax.ppermute(piece, "band", [(i, (i + shift) % 4) for i in range(4)])
+    turned = turned.reshape(4, local_slots, total_slots * 4)
+    rotated = jnp.zeros((local_slots, size_x, size_y, size_z), jnp.float32)
+
+    def put(rotated, piece, shift):
+        piece = piece.astype(jnp.float32).reshape(local_slots, 1, size_y, size_z)
+        return lax.dynamic_update_slice_in_dim(rotated, piece, lax.rem(band + 4 - shift, 4), 1)
+
+    def rows_for(shift):
+        return lax.dynamic_index_in_dim(turned, lax.rem(band + shift, 4), 0, keepdims=False)
+
+    rotated = put(rotated, rows_for(0), 0)
+    second, first, third = (to_band(rows_for(shift), shift) for shift in (2, 1, 3))
     gram = reduce_over(gram, "gx", 2, 4)
+    gram, second = lax.optimization_barrier((gram, second))
     gram = reduce_over(gram, "gyz", 2, 4)
-    back = lax.all_to_all(turned.reshape(4, local_slots, 1024), "band", 0, 0, tiled=True)
+    gram, first = lax.optimization_barrier((gram, first))
     gram = reduce_over(gram, "gyz", 1, 2)
-    gram, back = lax.optimization_barrier((gram, back))
-    rotated = jnp.swapaxes(back, 0, 1).reshape(local_slots, size_x, size_y, size_z)
-    rotated = rotated.astype(jnp.float32)
-    beyond = lax.ppermute(gram, "gx", ACROSS)
-    gram = (
-        jnp.concatenate(
-            [jnp.where(core == 0, gram, beyond), jnp.where(core == 0, beyond, gram)], axis=1
-        )
-        / total_cells
-    )
+    gram, third = lax.optimization_barrier((gram, third))
+    gram = gram + lax.ppermute(gram, "gx", ACROSS)
+    for shift, piece in ((2, second), (1, first), (3, third)):
+        rotated = put(rotated, piece, shift)
     return (gram, rotated)
 
 

time: 106 us -> 104 us (0.981)
  matrix products: 5.53 us -> 4.23 us
  starting transfers between devices: 34.9 us -> 33.8 us
    ppermute x12 -> x14, starting transfers between devices: 16.3 us -> 22.9 us  [the longest x6 11.4 us: to_band(): return lax.ppermute(value, 'band', [(i, (i + shift) % 4) for i in range(4)])]
    all_to_all x1 -> x0, starting transfers between devices: 6.21 us -> none  [on_device(): lax.all_to_all(turned.reshape(4, local_slots, 1024), 'band', 0, 0, tiled=...]
    all_to_all x1, starting transfers between devices: 12.1 us -> 10.7 us  [on_device(): lax.all_to_all(filtered.reshape(256, 8, 128), ('band', 'gx', 'gyz'), 0, 0...]
    convert_element_type x1, local copies, waits for them, and re-layouts: 1.12 us -> 0.02 us  [on_device(): gram = gram + to_band(piece.astype(jnp.bfloat16), shift).astype(jnp.float32)]
    ppermute x12 -> x14, waiting for transfers between devices: 9.05 us -> 9.03 us  [the longest x7 8.24 us: reduce_over(): total = total + lax.ppermute(sent, axis, pairs).astype(value.dtype)]
  transfers between devices with their start and end apart: 15 -> 16, of which waited for: 9 -> 9; matrix products, arithmetic and copies ran while one was open for 4% -> 3% of each run, Pallas kernels for 0% -> 0%
where the time goes in v3:
time: 104 us
  starting transfers between devices  33.8 us (32%)
  waiting for transfers between devices  29.7 us (29%)
  blocking collectives  25.5 us (25%)
  Pallas kernels  4.7 us (5%)
  matrix products  4.23 us (4%)
  local copies, waits for them, and re-layouts  2.52 us (2%)
  other arithmetic  2.05 us (2%)
  between operations  1.08 us (1%)
    all_to_all x1, blocking collectives, on_device(): taken = lax.all_to_all(message, ('gx', 'gyz'), 0, 0, tiled=True)  25.5 us
    all_to_all x1, waiting for transfers between devices, on_device(): lax.all_to_all(filtered.reshape(256, 8, 128), ('band', 'gx', 'gyz'), 0, 0...  20.7 us
    ppermute x6, starting transfers between devices, to_band(): return lax.ppermute(value, 'band', [(i, (i + shift) % 4) for i in range(4)])  11.4 us
    all_to_all x1, starting transfers between devices, on_device(): lax.all_to_all(filtered.reshape(256, 8, 128), ('band', 'gx', 'gyz'), 0, 0...  10.7 us
    ppermute x7, waiting for transfers between devices, reduce_over(): total = total + lax.ppermute(sent, axis, pairs).astype(value.dtype)  8.24 us
    ppermute x1, starting transfers between devices, on_device(): gram = gram + lax.ppermute(gram, 'gx', ACROSS)  5.86 us
    ppermute x7, starting transfers between devices, reduce_over(): total = total + lax.ppermute(sent, axis, pairs).astype(value.dtype)  5.64 us
    pallas_call x1, Pallas kernels, run_filter(): pl.pallas_call(filter_kernel, out_shape=jax.ShapeDtypeStruct((4, 8, NY, N...  4.7 us
  transfers between devices with their start and end apart: 16, of which 9 were waited for; matrix products, arithmetic and copies ran while one was open for 3% of the time, Pallas kernels for 0%

profile of v3, /device:TPU:1, one launch (start us, length us, event | category | flops | bytes accessed | tf_op | source)
XLA Modules:
  0.0 103.6 jit_solution(6754408585750007729)
XLA Ops:
  0.6 0.9 pad.4
  1.7 1.8 %fusion.1 = bf16[256,4096]{1,0:T(8,128)(2,1)S(1)} fusion(bf16[256,11]{0,1:T(8,128)(2,1)} %param.12, bf16[11,4096]{1,0:T(8,128)(2,1)S(1)} %bitcast.87), kind=kOutput, calls=%fused_computation.5 | convolution fusion | flops 27262976 | bytes 2192896 | tf_op jit(solution)/shard_map/dot_general | solution.py:37
  3.5 1.4 %convolution_bitcast_fusion = f32[8,4096]{1,0:T(8,128)S(1)} fusion(bf16[256,4096]{1,0:T(8,128)(2,1)S(1)} %fusion.1, bf16[1,256,256]{2,1,0:T(8,128)(2,1)S(1)} %copy-done, bf16[256]{0:T(256)(128)(2,1)S(1)} %copy-done.6), kind=kOutput, calls=%fused_computation.7 | convolution fusion | flops 557842432 | bytes 2359808 | tf_op jit(solution)/shard_map/dot_general | solution.py:40
  5.4 25.5 %all_to_all.10 = f16[64,6,8,128]{3,2,1,0:T(8,128)(2,1)S(1)} all-to-all(f16[64,6,8,128]{3,2,1,0:T(8,128)(2,1)S(1)} %pad_maximum_fusion), channel_id=1, replica_groups=mesh['gx'=8,'gyz'=8,'band'=4] {'gx','gyz'}, dimensions={0} | all-to-all | bytes 1572864 | tf_op jit(solution)/shard_map/all_to_all | solution.py:181
  31.2 0.6 dynamic_slice.30
  31.8 0.7 pad_add_fusion.info
  32.7 4.7 %shard_map.104 = bf16[4,8,64,128]{3,2,1,0:T(8,128)(2,1)} custom-call(s32[2]{0:T(128)S(1)} %pad_add_fusion.info, f32[64,6,8,128]{3,2,1,0:T(8,128)S(1)} %convert_element_type.101.taken, f32[64,2,8,128]{3,2,1,0:T(8,128)S(1)} %convert_element_type.102.other), custom_call_target="tpu_custom_call" | custom-call | flops 33554432 | bytes 3145728 | tf_op jit(solution)/shard_map/pallas_call | solution.py:130
  37.4 10.7 %all-to-all-start.1 = ((bf16[256,8,128]{2,1,0:T(8,128)(2,1)}), bf16[256,8,128]{2,1,0:T(8,128)(2,1)S(1)}, u32[]{:S(2)}, u32[]{:S(2)}) async-start(bf16[256,8,128]{2,1,0:T(8,128)(2,1)} %bitcast.7), calls=%async_computation.1 | async-start | bytes 1048576 | tf_op jit(solution)/shard_map/all_to_all | solution.py:193
  48.1 0.4 convolution_convert_fusion.1
  48.5 20.7 %all-to-all-done.1 = bf16[256,8,128]{2,1,0:T(8,128)(2,1)S(1)} async-done(((bf16[256,8,128]{2,1,0:T(8,128)(2,1)}), bf16[256,8,128]{2,1,0:T(8,128)(2,1)S(1)}, u32[]{:S(2)}, u32[]{:S(2)}) %all-to-all-start.1) | async-done | bytes 524320 | tf_op jit(solution)/shard_map/all_to_all | solution.py:193
  69.2 0.3 copy.17
  69.5 0.3 fusion.3
  69.9 0.9 collective-permute-start.3
  70.7 2.9 %collective-permute-start.2 = (bf16[64,256]{1,0:T(8,128)(2,1)S(1)}, bf16[64,256]{1,0:T(8,128)(2,1)S(1)}, u32[]{:S(2)}, u32[]{:S(2)}) collective-permute-start(bf16[64,256]{1,0:T(8,128)(2,1)S(1)} %get-tuple-element.24), channel_id=1, source_target_pairs={{0,2},{1,3},{2,0},{3,1},{4,6},{5,7},{6,4},{7,5},{8,10},{9,11},{10,... | collective-permute-start | bytes 98312 | tf_op jit(solution)/shard_map/ppermute | solution.py:160
  73.7 0.3 convolution_convert_fusion
  74.1 4.3 %collective-permute-start.7 = (bf16[64,1024]{1,0:T(8,128)(2,1)S(1)}, bf16[64,1024]{1,0:T(8,128)(2,1)S(1)}, u32[]{:S(2)}, u32[]{:S(2)}) collective-permute-start(bf16[64,1024]{1,0:T(8,128)(2,1)S(1)} %get-tuple-element.21), channel_id=1, source_target_pairs={{0,2},{1,3},{2,0},{3,1},{4,6},{5,7},{6,4},{7,5},{8,10},{9,11},{10,... | collective-permute-start | bytes 393224 | tf_op jit(solution)/shard_map/ppermute | solution.py:160
  78.4 1.5 %collective-permute-start.11 = (bf16[64,1024]{1,0:T(8,128)(2,1)S(1)}, bf16[64,1024]{1,0:T(8,128)(2,1)S(1)}, u32[]{:S(2)}, u32[]{:S(2)}) collective-permute-start(bf16[64,1024]{1,0:T(8,128)(2,1)S(1)} %get-tuple-element.20), channel_id=1, source_target_pairs={{0,1},{1,2},{2,3},{3,0},{4,5},{5,6},{6,7},{7,4},{8,9},{9,10},{10,1... | collective-permute-start | bytes 393224 | tf_op jit(solution)/shard_map/ppermute | solution.py:160
  79.9 1.3 %collective-permute-start.6 = (bf16[64,256]{1,0:T(8,128)(2,1)S(1)}, bf16[64,256]{1,0:T(8,128)(2,1)S(1)}, u32[]{:S(2)}, u32[]{:S(2)}) collective-permute-start(bf16[64,256]{1,0:T(8,128)(2,1)S(1)} %fusion.16), channel_id=1, source_target_pairs={{0,192},{32,224},{64,0},{96,32},{128,64},{160,96},{192,128},{224,1... | collective-permute-start | bytes 98312 | tf_op jit(solution)/shard_map/ppermute | solution.py:155
  81.3 0.8 collective-permute-start.5
  82.1 0.5 collective-permute-start.4
  82.7 0.4 collective-permute-done.6
  83.1 1.8 %collective-permute-start.13 = (bf16[64,1024]{1,0:T(8,128)(2,1)S(1)}, bf16[64,1024]{1,0:T(8,128)(2,1)S(1)}, u32[]{:S(2)}, u32[]{:S(2)}) collective-permute-start(bf16[64,1024]{1,0:T(8,128)(2,1)S(1)} %get-tuple-element.19), channel_id=1, source_target_pairs={{0,3},{1,0},{2,1},{3,2},{4,7},{5,4},{6,5},{7,6},{8,11},{9,8},{10,9... | collective-permute-start | bytes 393224 | tf_op jit(solution)/shard_map/ppermute | solution.py:160
  84.9 0.9 collective-permute-done.5
  85.8 0.4 collective-permute-done.4
  86.3 1.5 %collective-permute-start.10 = (bf16[64,256]{1,0:T(8,128)(2,1)S(1)}, bf16[64,256]{1,0:T(8,128)(2,1)S(1)}, u32[]{:S(2)}, u32[]{:S(2)}) collective-permute-start(bf16[64,256]{1,0:T(8,128)(2,1)S(1)} %convert_element_type.120), channel_id=1, source_target_pairs={{0,24},{4,28},{8,0},{12,4},{16,8},{20,12},{24,16},{28,20},{1,25},{... | collective-permute-start | bytes 98312 | tf_op jit(solution)/shard_map/ppermute | solution.py:155
  87.8 1.1 %collective-permute-start.9 = (bf16[64,256]{1,0:T(8,128)(2,1)S(1)}, bf16[64,256]{1,0:T(8,128)(2,1)S(1)}, u32[]{:S(2)}, u32[]{:S(2)}) collective-permute-start(bf16[64,256]{1,0:T(8,128)(2,1)S(1)} %convert_element_type.120), channel_id=1, source_target_pairs={{0,16},{4,20},{8,24},{12,28},{16,0},{20,4},{24,8},{28,12},{1,17},{... | collective-permute-start | bytes 98312 | tf_op jit(solution)/shard_map/ppermute | solution.py:155
  89.4 2.7 %collective-permute-done.9 = bf16[64,256]{1,0:T(8,128)(2,1)S(1)} collective-permute-done((bf16[64,256]{1,0:T(8,128)(2,1)S(1)}, bf16[64,256]{1,0:T(8,128)(2,1)S(1)}, u32[]{:S(2)}, u32[]{:S(2)}) %collective-permute-start.9) | collective-permute-done | bytes 32800 | tf_op jit(solution)/shard_map/ppermute | solution.py:155
  92.1 0.9 collective-permute-done.8
  93.3 2.8 %collective-permute-done.12 = bf16[64,256]{1,0:T(8,128)(2,1)S(1)} collective-permute-done((bf16[64,256]{1,0:T(8,128)(2,1)S(1)}, bf16[64,256]{1,0:T(8,128)(2,1)S(1)}, u32[]{:S(2)}, u32[]{:S(2)}) %collective-permute-start.12) | collective-permute-done | bytes 32800 | tf_op jit(solution)/shard_map/ppermute | solution.py:155
  96.2 5.9 %collective-permute-start.14 = (f32[64,256]{1,0:T(8,128)S(1)}, f32[64,256]{1,0:T(8,128)S(1)}, u32[]{:S(2)}, u32[]{:S(2)}) collective-permute-start(f32[64,256]{1,0:T(8,128)S(1)} %convert_add_fusion), channel_id=1, source_target_pairs={{0,32},{32,0},{64,96},{96,64},{128,160},{160,128},{192,224},{224,1... | collective-permute-start | bytes 196616 | tf_op jit(solution)/shard_map/ppermute | solution.py:228
  102.1 0.8 collective-permute-done.14
  102.9 0.6 add.126
  (57 shorter events, 2.2 us)
Async XLA Ops:
  0.6 2.8 %copy-start = (bf16[1,256,256]{2,1,0:T(8,128)(2,1)S(1)}, bf16[1,256,256]{2,1,0:T(8,128)(2,1)}, u32[]{:S(2)}) copy-start(bf16[1,256,256]{2,1,0:T(8,128)(2,1)} %param.13) | copy-start | bytes 393220
  1.6 1.8 %copy-start.6 = (bf16[256]{0:T(256)(128)(2,1)S(1)}, bf16[256]{0:T(256)(128)(2,1)}, u32[]{:S(2)}) copy-start(bf16[256]{0:T(256)(128)(2,1)} %param.14) | copy-start | bytes 1540
  3.5 1.5 %copy-start.1 = (f32[64,4,8,128]{3,2,1,0:T(8,128)S(1)}, f32[64,4,8,128]{3,2,1,0:T(8,128)}, u32[]{:S(2)}) copy-start(f32[64,4,8,128]{3,2,1,0:T(8,128)} %param.9) | copy-start | bytes 3145732
  3.5 1.6 %copy-start.4 = (f32[4,8,128]{2,1,0:T(8,128)S(1)}, f32[4,8,128]{2,1,0:T(8,128)}, u32[]{:S(2)}) copy-start(f32[4,8,128]{2,1,0:T(8,128)} %param.10) | copy-start | bytes 49156
  5.1 26.1 %copy-start.7 = (s32[64]{0:T(128)S(1)}, s32[64]{0:T(128)}, u32[]{:S(2)}) copy-start(s32[64]{0:T(128)} %param.17) | copy-start | bytes 772
  30.9 1.8 %collective-permute-start = (f16[64,2,8,128]{3,2,1,0:T(8,128)(2,1)S(1)}, f16[64,2,8,128]{3,2,1,0:T(8,128)(2,1)S(1)}, u32[]{:S(2)}, u32[]{:S(2)}) collective-permute-start(f16[64,2,8,128]{3,2,1,0:T(8,128)(2,1)S(1)} %slice.9), channel_id=1, source_target_pairs={{0,32},{32,0},{64,96},{96,64},{128,160},{160,128},{192,224},{224,1... | collective-permute-start | bytes 786440 | tf_op jit(solution)/shard_map/ppermute | solution.py:182
  32.6 15.5 %copy-start.3 = (f32[256,256]{1,0:T(8,128)S(1)}, f32[256,256]{1,0:T(8,128)}, u32[]{:S(2)}) copy-start(f32[256,256]{1,0:T(8,128)} %param.15) | copy-start | bytes 786436
  32.6 15.5 %copy-start.5 = (s32[256]{0:T(256)S(1)}, s32[256]{0:T(256)}, u32[]{:S(2)}) copy-start(s32[256]{0:T(256)} %param.16) | copy-start | bytes 3076
  37.4 31.8 %all-to-all-start.1 = ((bf16[256,8,128]{2,1,0:T(8,128)(2,1)}), bf16[256,8,128]{2,1,0:T(8,128)(2,1)S(1)}, u32[]{:S(2)}, u32[]{:S(2)}) async-start(bf16[256,8,128]{2,1,0:T(8,128)(2,1)} %bitcast.7), calls=%async_computation.1 | async-start | bytes 1048576 | tf_op jit(solution)/shard_map/all_to_all | solution.py:193
  69.9 10.0 %collective-permute-start.3 = (bf16[64,256]{1,0:T(8,128)(2,1)S(1)}, bf16[64,256]{1,0:T(8,128)(2,1)S(1)}, u32[]{:S(2)}, u32[]{:S(2)}) collective-permute-start(bf16[64,256]{1,0:T(8,128)(2,1)S(1)} %get-tuple-element.23), channel_id=1, source_target_pairs={{0,3},{1,0},{2,1},{3,2},{4,7},{5,4},{6,5},{7,6},{8,11},{9,8},{10,9... | collective-permute-start | bytes 98312 | tf_op jit(solution)/shard_map/ppermute | solution.py:160
  70.7 9.2 %collective-permute-start.2 = (bf16[64,256]{1,0:T(8,128)(2,1)S(1)}, bf16[64,256]{1,0:T(8,128)(2,1)S(1)}, u32[]{:S(2)}, u32[]{:S(2)}) collective-permute-start(bf16[64,256]{1,0:T(8,128)(2,1)S(1)} %get-tuple-element.24), channel_id=1, source_target_pairs={{0,2},{1,3},{2,0},{3,1},{4,6},{5,7},{6,4},{7,5},{8,10},{9,11},{10,... | collective-permute-start | bytes 98312 | tf_op jit(solution)/shard_map/ppermute | solution.py:160
  73.7 6.2 %collective-permute-start.1 = (bf16[64,256]{1,0:T(8,128)(2,1)S(1)}, bf16[64,256]{1,0:T(8,128)(2,1)S(1)}, u32[]{:S(2)}, u32[]{:S(2)}) collective-permute-start(bf16[64,256]{1,0:T(8,128)(2,1)S(1)} %get-tuple-element.22), channel_id=1, source_target_pairs={{0,1},{1,2},{2,3},{3,0},{4,5},{5,6},{6,7},{7,4},{8,9},{9,10},{10,1... | collective-permute-start | bytes 98312 | tf_op jit(solution)/shard_map/ppermute | solution.py:160
  74.1 12.2 %collective-permute-start.7 = (bf16[64,1024]{1,0:T(8,128)(2,1)S(1)}, bf16[64,1024]{1,0:T(8,128)(2,1)S(1)}, u32[]{:S(2)}, u32[]{:S(2)}) collective-permute-start(bf16[64,1024]{1,0:T(8,128)(2,1)S(1)} %get-tuple-element.21), channel_id=1, source_target_pairs={{0,2},{1,3},{2,0},{3,1},{4,6},{5,7},{6,4},{7,5},{8,10},{9,11},{10,... | collective-permute-start | bytes 393224 | tf_op jit(solution)/shard_map/ppermute | solution.py:160
  78.4 14.6 %collective-permute-start.11 = (bf16[64,1024]{1,0:T(8,128)(2,1)S(1)}, bf16[64,1024]{1,0:T(8,128)(2,1)S(1)}, u32[]{:S(2)}, u32[]{:S(2)}) collective-permute-start(bf16[64,1024]{1,0:T(8,128)(2,1)S(1)} %get-tuple-element.20), channel_id=1, source_target_pairs={{0,1},{1,2},{2,3},{3,0},{4,5},{5,6},{6,7},{7,4},{8,9},{9,10},{10,1... | collective-permute-start | bytes 393224 | tf_op jit(solution)/shard_map/ppermute | solution.py:160
  79.9 3.1 %collective-permute-start.6 = (bf16[64,256]{1,0:T(8,128)(2,1)S(1)}, bf16[64,256]{1,0:T(8,128)(2,1)S(1)}, u32[]{:S(2)}, u32[]{:S(2)}) collective-permute-start(bf16[64,256]{1,0:T(8,128)(2,1)S(1)} %fusion.16), channel_id=1, source_target_pairs={{0,192},{32,224},{64,0},{96,32},{128,64},{160,96},{192,128},{224,1... | collective-permute-start | bytes 98312 | tf_op jit(solution)/shard_map/ppermute | solution.py:155
  81.3 4.6 %collective-permute-start.5 = (bf16[64,256]{1,0:T(8,128)(2,1)S(1)}, bf16[64,256]{1,0:T(8,128)(2,1)S(1)}, u32[]{:S(2)}, u32[]{:S(2)}) collective-permute-start(bf16[64,256]{1,0:T(8,128)(2,1)S(1)} %fusion.16), channel_id=1, source_target_pairs={{0,128},{32,160},{64,192},{96,224},{128,0},{160,32},{192,64},{224,... | collective-permute-start | bytes 98312 | tf_op jit(solution)/shard_map/ppermute | solution.py:155
  82.1 4.1 %collective-permute-start.4 = (bf16[64,256]{1,0:T(8,128)(2,1)S(1)}, bf16[64,256]{1,0:T(8,128)(2,1)S(1)}, u32[]{:S(2)}, u32[]{:S(2)}) collective-permute-start(bf16[64,256]{1,0:T(8,128)(2,1)S(1)} %fusion.16), channel_id=1, source_target_pairs={{0,64},{32,96},{64,128},{96,160},{128,192},{160,224},{192,0},{224,... | collective-permute-start | bytes 98312 | tf_op jit(solution)/shard_map/ppermute | solution.py:155
  83.1 13.1 %collective-permute-start.13 = (bf16[64,1024]{1,0:T(8,128)(2,1)S(1)}, bf16[64,1024]{1,0:T(8,128)(2,1)S(1)}, u32[]{:S(2)}, u32[]{:S(2)}) collective-permute-start(bf16[64,1024]{1,0:T(8,128)(2,1)S(1)} %get-tuple-element.19), channel_id=1, source_target_pairs={{0,3},{1,0},{2,1},{3,2},{4,7},{5,4},{6,5},{7,6},{8,11},{9,8},{10,9... | collective-permute-start | bytes 393224 | tf_op jit(solution)/shard_map/ppermute | solution.py:160
  86.3 3.1 %collective-permute-start.10 = (bf16[64,256]{1,0:T(8,128)(2,1)S(1)}, bf16[64,256]{1,0:T(8,128)(2,1)S(1)}, u32[]{:S(2)}, u32[]{:S(2)}) collective-permute-start(bf16[64,256]{1,0:T(8,128)(2,1)S(1)} %convert_element_type.120), channel_id=1, source_target_pairs={{0,24},{4,28},{8,0},{12,4},{16,8},{20,12},{24,16},{28,20},{1,25},{... | collective-permute-start | bytes 98312 | tf_op jit(solution)/shard_map/ppermute | solution.py:155
  87.8 4.3 %collective-permute-start.9 = (bf16[64,256]{1,0:T(8,128)(2,1)S(1)}, bf16[64,256]{1,0:T(8,128)(2,1)S(1)}, u32[]{:S(2)}, u32[]{:S(2)}) collective-permute-start(bf16[64,256]{1,0:T(8,128)(2,1)S(1)} %convert_element_type.120), channel_id=1, source_target_pairs={{0,16},{4,20},{8,24},{12,28},{16,0},{20,4},{24,8},{28,12},{1,17},{... | collective-permute-start | bytes 98312 | tf_op jit(solution)/shard_map/ppermute | solution.py:155
  89.0 4.0 %collective-permute-start.8 = (bf16[64,256]{1,0:T(8,128)(2,1)S(1)}, bf16[64,256]{1,0:T(8,128)(2,1)S(1)}, u32[]{:S(2)}, u32[]{:S(2)}) collective-permute-start(bf16[64,256]{1,0:T(8,128)(2,1)S(1)} %convert_element_type.120), channel_id=1, source_target_pairs={{0,8},{4,12},{8,16},{12,20},{16,24},{20,28},{24,0},{28,4},{1,9},{5... | collective-permute-start | bytes 98312 | tf_op jit(solution)/shard_map/ppermute | solution.py:155
  93.0 3.1 %collective-permute-start.12 = (bf16[64,256]{1,0:T(8,128)(2,1)S(1)}, bf16[64,256]{1,0:T(8,128)(2,1)S(1)}, u32[]{:S(2)}, u32[]{:S(2)}) collective-permute-start(bf16[64,256]{1,0:T(8,128)(2,1)S(1)} %convert_element_type.124), channel_id=1, source_target_pairs={{0,4},{4,0},{8,12},{12,8},{16,20},{20,16},{24,28},{28,24},{1,5},{5... | collective-permute-start | bytes 98312 | tf_op jit(solution)/shard_map/ppermute | solution.py:155
  96.2 6.8 %collective-permute-start.14 = (f32[64,256]{1,0:T(8,128)S(1)}, f32[64,256]{1,0:T(8,128)S(1)}, u32[]{:S(2)}, u32[]{:S(2)}) collective-permute-start(f32[64,256]{1,0:T(8,128)S(1)} %convert_add_fusion), channel_id=1, source_target_pairs={{0,32},{32,0},{64,96},{96,64},{128,160},{160,128},{192,224},{224,1... | collective-permute-start | bytes 196616 | tf_op jit(solution)/shard_map/ppermute | solution.py:228
  102.1 1.4 %copy-start.2 = (f32[64,4,8,128]{3,2,1,0:T(8,128)}, f32[64,4,8,128]{3,2,1,0:T(8,128)S(1)}, u32[]{:S(2)}) copy-start(f32[64,4,8,128]{3,2,1,0:T(8,128)S(1)} %constant_dynamic-update-slice_fusion) | copy-start | bytes 3145732

commit v4 on v3

--- a/solution.py
+++ b/solution.py
@@ -218,9 +218,12 @@
         return lax.dynamic_index_in_dim(turned, lax.rem(band + shift, 4), 0, keepdims=False)
 
     rotated = put(rotated, rows_for(0), 0)
-    second, first, third = (to_band(rows_for(shift), shift) for shift in (2, 1, 3))
+    second = to_band(rows_for(2), 2)
+    gram, leaving = lax.optimization_barrier((gram, rows_for(1)))
+    first = to_band(leaving, 1)
     gram = reduce_over(gram, "gx", 2, 4)
-    gram, second = lax.optimization_barrier((gram, second))
+    gram, second, leaving = lax.optimization_barrier((gram, second, rows_for(3)))
+    third = to_band(leaving, 3)
     gram = reduce_over(gram, "gyz", 2, 4)
     gram, first = lax.optimization_barrier((gram, first))
     gram = reduce_over(gram, "gyz", 1, 2)

time: 104 us -> 104 us (level)
  starting transfers between devices: 33.8 us -> 32.5 us
  Pallas kernels: 4.7 us -> 5.91 us
    ppermute x1, starting transfers between devices: 5.86 us -> 2.47 us  [on_device(): gram = gram + lax.ppermute(gram, 'gx', ACROSS)]
    ppermute x6, starting transfers between devices: 11.4 us -> 14.5 us  [to_band(): return lax.ppermute(value, 'band', [(i, (i + shift) % 4) for i in range(4)])]
    pallas_call x1, Pallas kernels: 4.7 us -> 5.91 us  [run_filter(): pl.pallas_call(filter_kernel, out_shape=jax.ShapeDtypeStruct((4, 8, NY, N...]
  transfers between devices with their start and end apart: 16 -> 16, of which waited for: 9 -> 6; matrix products, arithmetic and copies ran while one was open for 3% -> 3% of each run, Pallas kernels for 0% -> 0%
where the time goes in v4:
time: 104 us; the launch traced here: 103 us
  starting transfers between devices  32.5 us (31%)
  waiting for transfers between devices  29.6 us (28%)
  blocking collectives  25.5 us (25%)
  Pallas kernels  5.91 us (6%)
  matrix products  4.23 us (4%)
  local copies, waits for them, and re-layouts  2.52 us (2%)
  other arithmetic  2.05 us (2%)
  between operations  1.1 us (1%)
    all_to_all x1, blocking collectives, on_device(): taken = lax.all_to_all(message, ('gx', 'gyz'), 0, 0, tiled=True)  25.5 us
    all_to_all x1, waiting for transfers between devices, on_device(): lax.all_to_all(filtered.reshape(256, 8, 128), ('band', 'gx', 'gyz'), 0, 0...  20.7 us
    ppermute x6, starting transfers between devices, to_band(): return lax.ppermute(value, 'band', [(i, (i + shift) % 4) for i in range(4)])  14.5 us
    all_to_all x1, starting transfers between devices, on_device(): lax.all_to_all(filtered.reshape(256, 8, 128), ('band', 'gx', 'gyz'), 0, 0...  9.95 us
    ppermute x7, waiting for transfers between devices, reduce_over(): total = total + lax.ppermute(sent, axis, pairs).astype(value.dtype)  7.61 us
    pallas_call x1, Pallas kernels, run_filter(): pl.pallas_call(filter_kernel, out_shape=jax.ShapeDtypeStruct((4, 8, NY, N...  5.91 us
    ppermute x7, starting transfers between devices, reduce_over(): total = total + lax.ppermute(sent, axis, pairs).astype(value.dtype)  5.28 us
    ppermute x1, starting transfers between devices, on_device(): gram = gram + lax.ppermute(gram, 'gx', ACROSS)  2.47 us
  transfers between devices with their start and end apart: 16, of which 6 were waited for; matrix products, arithmetic and copies ran while one was open for 3% of the time, Pallas kernels for 0%

profile of v4, /device:TPU:1, one launch (start us, length us, event | category | flops | bytes accessed | tf_op | source)
XLA Modules:
  0.0 103.3 jit_solution(3155808521487259862)
XLA Ops:
  0.6 0.9 pad.4
  1.7 1.8 %fusion.1 = bf16[256,4096]{1,0:T(8,128)(2,1)S(1)} fusion(bf16[256,11]{0,1:T(8,128)(2,1)} %param.12, bf16[11,4096]{1,0:T(8,128)(2,1)S(1)} %bitcast.80), kind=kOutput, calls=%fused_computation.5 | convolution fusion | flops 27262976 | bytes 2192896 | tf_op jit(solution)/shard_map/dot_general | solution.py:37
  3.5 1.4 %convolution_bitcast_fusion = f32[8,4096]{1,0:T(8,128)S(1)} fusion(bf16[256,4096]{1,0:T(8,128)(2,1)S(1)} %fusion.1, bf16[1,256,256]{2,1,0:T(8,128)(2,1)S(1)} %copy-done, bf16[256]{0:T(256)(128)(2,1)S(1)} %copy-done.6), kind=kOutput, calls=%fused_computation.7 | convolution fusion | flops 557842432 | bytes 2359808 | tf_op jit(solution)/shard_map/dot_general | solution.py:40
  5.4 25.5 %all_to_all.10 = f16[64,6,8,128]{3,2,1,0:T(8,128)(2,1)S(1)} all-to-all(f16[64,6,8,128]{3,2,1,0:T(8,128)(2,1)S(1)} %pad_maximum_fusion), channel_id=1, replica_groups=mesh['gx'=8,'gyz'=8,'band'=4] {'gx','gyz'}, dimensions={0} | all-to-all | bytes 1572864 | tf_op jit(solution)/shard_map/all_to_all | solution.py:181
  30.9 0.3 collective-permute-start
  31.2 0.6 dynamic_slice.30
  31.8 0.7 pad_add_fusion.info
  32.7 5.9 %shard_map.104 = bf16[4,8,64,128]{3,2,1,0:T(8,128)(2,1)} custom-call(s32[2]{0:T(128)S(1)} %pad_add_fusion.info, f32[64,6,8,128]{3,2,1,0:T(8,128)S(1)} %convert_element_type.101.taken, f32[64,2,8,128]{3,2,1,0:T(8,128)S(1)} %convert_element_type.102.other), custom_call_target="tpu_custom_call" | custom-call | flops 33554432 | bytes 3145728 | tf_op jit(solution)/shard_map/pallas_call | solution.py:130
  38.6 10.0 %all-to-all-start.1 = ((bf16[256,8,128]{2,1,0:T(8,128)(2,1)}), bf16[256,8,128]{2,1,0:T(8,128)(2,1)S(1)}, u32[]{:S(2)}, u32[]{:S(2)}) async-start(bf16[256,8,128]{2,1,0:T(8,128)(2,1)} %bitcast.7), calls=%async_computation.1 | async-start | bytes 1048576 | tf_op jit(solution)/shard_map/all_to_all | solution.py:193
  48.6 0.4 convolution_convert_fusion.1
  49.0 20.7 %all-to-all-done.1 = bf16[256,8,128]{2,1,0:T(8,128)(2,1)S(1)} async-done(((bf16[256,8,128]{2,1,0:T(8,128)(2,1)}), bf16[256,8,128]{2,1,0:T(8,128)(2,1)S(1)}, u32[]{:S(2)}, u32[]{:S(2)}) %all-to-all-start.1) | async-done | bytes 524320 | tf_op jit(solution)/shard_map/all_to_all | solution.py:193
  69.7 0.3 copy.17
  70.0 0.3 fusion.3
  70.4 0.9 collective-permute-start.3
  71.2 2.9 %collective-permute-start.2 = (bf16[64,256]{1,0:T(8,128)(2,1)S(1)}, bf16[64,256]{1,0:T(8,128)(2,1)S(1)}, u32[]{:S(2)}, u32[]{:S(2)}) collective-permute-start(bf16[64,256]{1,0:T(8,128)(2,1)S(1)} %get-tuple-element.30), channel_id=1, source_target_pairs={{0,2},{1,3},{2,0},{3,1},{4,6},{5,7},{6,4},{7,5},{8,10},{9,11},{10,... | collective-permute-start | bytes 98312 | tf_op jit(solution)/shard_map/ppermute | solution.py:160
  74.2 0.4 convolution_convert_fusion
  74.6 4.3 %collective-permute-start.7 = (bf16[64,1024]{1,0:T(8,128)(2,1)S(1)}, bf16[64,1024]{1,0:T(8,128)(2,1)S(1)}, u32[]{:S(2)}, u32[]{:S(2)}) collective-permute-start(bf16[64,1024]{1,0:T(8,128)(2,1)S(1)} %get-tuple-element.26), channel_id=1, source_target_pairs={{0,2},{1,3},{2,0},{3,1},{4,6},{5,7},{6,4},{7,5},{8,10},{9,11},{10,... | collective-permute-start | bytes 393224 | tf_op jit(solution)/shard_map/ppermute | solution.py:160
  79.0 0.5 collective-permute-done.1
  79.5 1.1 %collective-permute-start.6 = (bf16[64,256]{1,0:T(8,128)(2,1)S(1)}, bf16[64,256]{1,0:T(8,128)(2,1)S(1)}, u32[]{:S(2)}, u32[]{:S(2)}) collective-permute-start(bf16[64,256]{1,0:T(8,128)(2,1)S(1)} %convert_element_type.116), channel_id=1, source_target_pairs={{0,192},{32,224},{64,0},{96,32},{128,64},{160,96},{192,128},{224,1... | collective-permute-start | bytes 98312 | tf_op jit(solution)/shard_map/ppermute | solution.py:155
  80.6 0.8 collective-permute-start.5
  81.4 0.5 collective-permute-start.4
  82.0 1.3 %collective-permute-start.11 = (bf16[64,1024]{1,0:T(8,128)(2,1)S(1)}, bf16[64,1024]{1,0:T(8,128)(2,1)S(1)}, u32[]{:S(2)}, u32[]{:S(2)}) collective-permute-start(bf16[64,1024]{1,0:T(8,128)(2,1)S(1)} %get-tuple-element.17), channel_id=1, source_target_pairs={{0,1},{1,2},{2,3},{3,0},{4,5},{5,6},{6,7},{7,4},{8,9},{9,10},{10,1... | collective-permute-start | bytes 393224 | tf_op jit(solution)/shard_map/ppermute | solution.py:160
  83.3 1.9 %collective-permute-done.5 = bf16[64,256]{1,0:T(8,128)(2,1)S(1)} collective-permute-done((bf16[64,256]{1,0:T(8,128)(2,1)S(1)}, bf16[64,256]{1,0:T(8,128)(2,1)S(1)}, u32[]{:S(2)}, u32[]{:S(2)}) %collective-permute-start.5) | collective-permute-done | bytes 32800 | tf_op jit(solution)/shard_map/ppermute | solution.py:155
  85.2 0.3 collective-permute-done.4
  85.6 1.6 %collective-permute-start.10 = (bf16[64,256]{1,0:T(8,128)(2,1)S(1)}, bf16[64,256]{1,0:T(8,128)(2,1)S(1)}, u32[]{:S(2)}, u32[]{:S(2)}) collective-permute-start(bf16[64,256]{1,0:T(8,128)(2,1)S(1)} %convert_element_type.120), channel_id=1, source_target_pairs={{0,24},{4,28},{8,0},{12,4},{16,8},{20,12},{24,16},{28,20},{1,25},{... | collective-permute-start | bytes 98312 | tf_op jit(solution)/shard_map/ppermute | solution.py:155
  87.2 0.7 collective-permute-start.9
  88.1 5.1 %collective-permute-start.13 = (bf16[64,1024]{1,0:T(8,128)(2,1)S(1)}, bf16[64,1024]{1,0:T(8,128)(2,1)S(1)}, u32[]{:S(2)}, u32[]{:S(2)}) collective-permute-start(bf16[64,1024]{1,0:T(8,128)(2,1)S(1)} %get-tuple-element.19), channel_id=1, source_target_pairs={{0,3},{1,0},{2,1},{3,2},{4,7},{5,4},{6,5},{7,6},{8,11},{9,8},{10,9... | collective-permute-start | bytes 393224 | tf_op jit(solution)/shard_map/ppermute | solution.py:160
  93.4 0.4 collective-permute-start.12
  93.9 5.4 %collective-permute-done.12 = bf16[64,256]{1,0:T(8,128)(2,1)S(1)} collective-permute-done((bf16[64,256]{1,0:T(8,128)(2,1)S(1)}, bf16[64,256]{1,0:T(8,128)(2,1)S(1)}, u32[]{:S(2)}, u32[]{:S(2)}) %collective-permute-start.12) | collective-permute-done | bytes 32800 | tf_op jit(solution)/shard_map/ppermute | solution.py:155
  99.3 2.5 %collective-permute-start.14 = (f32[64,256]{1,0:T(8,128)S(1)}, f32[64,256]{1,0:T(8,128)S(1)}, u32[]{:S(2)}, u32[]{:S(2)}) collective-permute-start(f32[64,256]{1,0:T(8,128)S(1)} %convert_add_fusion), channel_id=1, source_target_pairs={{0,32},{32,0},{64,96},{96,64},{128,160},{160,128},{192,224},{224,1... | collective-permute-start | bytes 196616 | tf_op jit(solution)/shard_map/ppermute | solution.py:231
  101.9 0.8 collective-permute-done.14
  102.7 0.6 add.126
  (58 shorter events, 1.5 us)
Async XLA Ops:
  0.6 2.8 %copy-start = (bf16[1,256,256]{2,1,0:T(8,128)(2,1)S(1)}, bf16[1,256,256]{2,1,0:T(8,128)(2,1)}, u32[]{:S(2)}) copy-start(bf16[1,256,256]{2,1,0:T(8,128)(2,1)} %param.13) | copy-start | bytes 393220
  1.6 1.8 %copy-start.6 = (bf16[256]{0:T(256)(128)(2,1)S(1)}, bf16[256]{0:T(256)(128)(2,1)}, u32[]{:S(2)}) copy-start(bf16[256]{0:T(256)(128)(2,1)} %param.14) | copy-start | bytes 1540
  3.5 1.5 %copy-start.1 = (f32[64,4,8,128]{3,2,1,0:T(8,128)S(1)}, f32[64,4,8,128]{3,2,1,0:T(8,128)}, u32[]{:S(2)}) copy-start(f32[64,4,8,128]{3,2,1,0:T(8,128)} %param.9) | copy-start | bytes 3145732
  3.5 1.6 %copy-start.4 = (f32[4,8,128]{2,1,0:T(8,128)S(1)}, f32[4,8,128]{2,1,0:T(8,128)}, u32[]{:S(2)}) copy-start(f32[4,8,128]{2,1,0:T(8,128)} %param.10) | copy-start | bytes 49156
  5.1 26.1 %copy-start.7 = (s32[64]{0:T(128)S(1)}, s32[64]{0:T(128)}, u32[]{:S(2)}) copy-start(s32[64]{0:T(128)} %param.17) | copy-start | bytes 772
  30.9 1.8 %collective-permute-start = (f16[64,2,8,128]{3,2,1,0:T(8,128)(2,1)S(1)}, f16[64,2,8,128]{3,2,1,0:T(8,128)(2,1)S(1)}, u32[]{:S(2)}, u32[]{:S(2)}) collective-permute-start(f16[64,2,8,128]{3,2,1,0:T(8,128)(2,1)S(1)} %slice.9), channel_id=1, source_target_pairs={{0,32},{32,0},{64,96},{96,64},{128,160},{160,128},{192,224},{224,1... | collective-permute-start | bytes 786440 | tf_op jit(solution)/shard_map/ppermute | solution.py:182
  32.6 16.0 %copy-start.3 = (f32[256,256]{1,0:T(8,128)S(1)}, f32[256,256]{1,0:T(8,128)}, u32[]{:S(2)}) copy-start(f32[256,256]{1,0:T(8,128)} %param.15) | copy-start | bytes 786436
  32.6 16.0 %copy-start.5 = (s32[256]{0:T(256)S(1)}, s32[256]{0:T(256)}, u32[]{:S(2)}) copy-start(s32[256]{0:T(256)} %param.16) | copy-start | bytes 3076
  38.6 31.0 %all-to-all-start.1 = ((bf16[256,8,128]{2,1,0:T(8,128)(2,1)}), bf16[256,8,128]{2,1,0:T(8,128)(2,1)S(1)}, u32[]{:S(2)}, u32[]{:S(2)}) async-start(bf16[256,8,128]{2,1,0:T(8,128)(2,1)} %bitcast.7), calls=%async_computation.1 | async-start | bytes 1048576 | tf_op jit(solution)/shard_map/all_to_all | solution.py:193
  70.4 8.6 %collective-permute-start.3 = (bf16[64,256]{1,0:T(8,128)(2,1)S(1)}, bf16[64,256]{1,0:T(8,128)(2,1)S(1)}, u32[]{:S(2)}, u32[]{:S(2)}) collective-permute-start(bf16[64,256]{1,0:T(8,128)(2,1)S(1)} %get-tuple-element.29), channel_id=1, source_target_pairs={{0,3},{1,0},{2,1},{3,2},{4,7},{5,4},{6,5},{7,6},{8,11},{9,8},{10,9... | collective-permute-start | bytes 98312 | tf_op jit(solution)/shard_map/ppermute | solution.py:160
  71.2 7.7 %collective-permute-start.2 = (bf16[64,256]{1,0:T(8,128)(2,1)S(1)}, bf16[64,256]{1,0:T(8,128)(2,1)S(1)}, u32[]{:S(2)}, u32[]{:S(2)}) collective-permute-start(bf16[64,256]{1,0:T(8,128)(2,1)S(1)} %get-tuple-element.30), channel_id=1, source_target_pairs={{0,2},{1,3},{2,0},{3,1},{4,6},{5,7},{6,4},{7,5},{8,10},{9,11},{10,... | collective-permute-start | bytes 98312 | tf_op jit(solution)/shard_map/ppermute | solution.py:160
  74.2 5.3 %collective-permute-start.1 = (bf16[64,256]{1,0:T(8,128)(2,1)S(1)}, bf16[64,256]{1,0:T(8,128)(2,1)S(1)}, u32[]{:S(2)}, u32[]{:S(2)}) collective-permute-start(bf16[64,256]{1,0:T(8,128)(2,1)S(1)} %get-tuple-element.28), channel_id=1, source_target_pairs={{0,1},{1,2},{2,3},{3,0},{4,5},{5,6},{6,7},{7,4},{8,9},{9,10},{10,1... | collective-permute-start | bytes 98312 | tf_op jit(solution)/shard_map/ppermute | solution.py:160
  74.6 11.0 %collective-permute-start.7 = (bf16[64,1024]{1,0:T(8,128)(2,1)S(1)}, bf16[64,1024]{1,0:T(8,128)(2,1)S(1)}, u32[]{:S(2)}, u32[]{:S(2)}) collective-permute-start(bf16[64,1024]{1,0:T(8,128)(2,1)S(1)} %get-tuple-element.26), channel_id=1, source_target_pairs={{0,2},{1,3},{2,0},{3,1},{4,6},{5,7},{6,4},{7,5},{8,10},{9,11},{10,... | collective-permute-start | bytes 393224 | tf_op jit(solution)/shard_map/ppermute | solution.py:160
  79.5 3.8 %collective-permute-start.6 = (bf16[64,256]{1,0:T(8,128)(2,1)S(1)}, bf16[64,256]{1,0:T(8,128)(2,1)S(1)}, u32[]{:S(2)}, u32[]{:S(2)}) collective-permute-start(bf16[64,256]{1,0:T(8,128)(2,1)S(1)} %convert_element_type.116), channel_id=1, source_target_pairs={{0,192},{32,224},{64,0},{96,32},{128,64},{160,96},{192,128},{224,1... | collective-permute-start | bytes 98312 | tf_op jit(solution)/shard_map/ppermute | solution.py:155
  80.6 4.6 %collective-permute-start.5 = (bf16[64,256]{1,0:T(8,128)(2,1)S(1)}, bf16[64,256]{1,0:T(8,128)(2,1)S(1)}, u32[]{:S(2)}, u32[]{:S(2)}) collective-permute-start(bf16[64,256]{1,0:T(8,128)(2,1)S(1)} %convert_element_type.116), channel_id=1, source_target_pairs={{0,128},{32,160},{64,192},{96,224},{128,0},{160,32},{192,64},{224,... | collective-permute-start | bytes 98312 | tf_op jit(solution)/shard_map/ppermute | solution.py:155
  81.4 4.1 %collective-permute-start.4 = (bf16[64,256]{1,0:T(8,128)(2,1)S(1)}, bf16[64,256]{1,0:T(8,128)(2,1)S(1)}, u32[]{:S(2)}, u32[]{:S(2)}) collective-permute-start(bf16[64,256]{1,0:T(8,128)(2,1)S(1)} %convert_element_type.116), channel_id=1, source_target_pairs={{0,64},{32,96},{64,128},{96,160},{128,192},{160,224},{192,0},{224,... | collective-permute-start | bytes 98312 | tf_op jit(solution)/shard_map/ppermute | solution.py:155
  82.0 11.3 %collective-permute-start.11 = (bf16[64,1024]{1,0:T(8,128)(2,1)S(1)}, bf16[64,1024]{1,0:T(8,128)(2,1)S(1)}, u32[]{:S(2)}, u32[]{:S(2)}) collective-permute-start(bf16[64,1024]{1,0:T(8,128)(2,1)S(1)} %get-tuple-element.17), channel_id=1, source_target_pairs={{0,1},{1,2},{2,3},{3,0},{4,5},{5,6},{6,7},{7,4},{8,9},{9,10},{10,1... | collective-permute-start | bytes 393224 | tf_op jit(solution)/shard_map/ppermute | solution.py:160
  85.6 7.7 %collective-permute-start.10 = (bf16[64,256]{1,0:T(8,128)(2,1)S(1)}, bf16[64,256]{1,0:T(8,128)(2,1)S(1)}, u32[]{:S(2)}, u32[]{:S(2)}) collective-permute-start(bf16[64,256]{1,0:T(8,128)(2,1)S(1)} %convert_element_type.120), channel_id=1, source_target_pairs={{0,24},{4,28},{8,0},{12,4},{16,8},{20,12},{24,16},{28,20},{1,25},{... | collective-permute-start | bytes 98312 | tf_op jit(solution)/shard_map/ppermute | solution.py:155
  87.2 6.1 %collective-permute-start.9 = (bf16[64,256]{1,0:T(8,128)(2,1)S(1)}, bf16[64,256]{1,0:T(8,128)(2,1)S(1)}, u32[]{:S(2)}, u32[]{:S(2)}) collective-permute-start(bf16[64,256]{1,0:T(8,128)(2,1)S(1)} %convert_element_type.120), channel_id=1, source_target_pairs={{0,16},{4,20},{8,24},{12,28},{16,0},{20,4},{24,8},{28,12},{1,17},{... | collective-permute-start | bytes 98312 | tf_op jit(solution)/shard_map/ppermute | solution.py:155
  87.9 5.4 %collective-permute-start.8 = (bf16[64,256]{1,0:T(8,128)(2,1)S(1)}, bf16[64,256]{1,0:T(8,128)(2,1)S(1)}, u32[]{:S(2)}, u32[]{:S(2)}) collective-permute-start(bf16[64,256]{1,0:T(8,128)(2,1)S(1)} %convert_element_type.120), channel_id=1, source_target_pairs={{0,8},{4,12},{8,16},{12,20},{16,24},{20,28},{24,0},{28,4},{1,9},{5... | collective-permute-start | bytes 98312 | tf_op jit(solution)/shard_map/ppermute | solution.py:155
  88.1 11.2 %collective-permute-start.13 = (bf16[64,1024]{1,0:T(8,128)(2,1)S(1)}, bf16[64,1024]{1,0:T(8,128)(2,1)S(1)}, u32[]{:S(2)}, u32[]{:S(2)}) collective-permute-start(bf16[64,1024]{1,0:T(8,128)(2,1)S(1)} %get-tuple-element.19), channel_id=1, source_target_pairs={{0,3},{1,0},{2,1},{3,2},{4,7},{5,4},{6,5},{7,6},{8,11},{9,8},{10,9... | collective-permute-start | bytes 393224 | tf_op jit(solution)/shard_map/ppermute | solution.py:160
  93.4 5.9 %collective-permute-start.12 = (bf16[64,256]{1,0:T(8,128)(2,1)S(1)}, bf16[64,256]{1,0:T(8,128)(2,1)S(1)}, u32[]{:S(2)}, u32[]{:S(2)}) collective-permute-start(bf16[64,256]{1,0:T(8,128)(2,1)S(1)} %convert_element_type.124), channel_id=1, source_target_pairs={{0,4},{4,0},{8,12},{12,8},{16,20},{20,16},{24,28},{28,24},{1,5},{5... | collective-permute-start | bytes 98312 | tf_op jit(solution)/shard_map/ppermute | solution.py:155
  99.3 3.4 %collective-permute-start.14 = (f32[64,256]{1,0:T(8,128)S(1)}, f32[64,256]{1,0:T(8,128)S(1)}, u32[]{:S(2)}, u32[]{:S(2)}) collective-permute-start(f32[64,256]{1,0:T(8,128)S(1)} %convert_add_fusion), channel_id=1, source_target_pairs={{0,32},{32,0},{64,96},{96,64},{128,160},{160,128},{192,224},{224,1... | collective-permute-start | bytes 196616 | tf_op jit(solution)/shard_map/ppermute | solution.py:231
  101.9 1.4 %copy-start.2 = (f32[64,4,8,128]{3,2,1,0:T(8,128)}, f32[64,4,8,128]{3,2,1,0:T(8,128)S(1)}, u32[]{:S(2)}) copy-start(f32[64,4,8,128]{3,2,1,0:T(8,128)S(1)} %constant_dynamic-update-slice_fusion) | copy-start | bytes 3145732

commit v5 on v4

--- a/solution.py
+++ b/solution.py
@@ -226,9 +226,12 @@
     third = to_band(leaving, 3)
     gram = reduce_over(gram, "gyz", 2, 4)
     gram, first = lax.optimization_barrier((gram, first))
-    gram = reduce_over(gram, "gyz", 1, 2)
-    gram, third = lax.optimization_barrier((gram, third))
-    gram = gram + lax.ppermute(gram, "gx", ACROSS)
+    sent = gram.astype(jnp.bfloat16)
+    others = [
+        lax.ppermute(sent, ("gx", "gyz"), [(i, i ^ flip) for i in range(64)]) for flip in (9, 1, 8)
+    ]
+    others[0], third = lax.optimization_barrier((others[0], third))
+    gram = gram + sum(other.astype(jnp.float32) for other in others)
     for shift, piece in ((2, second), (1, first), (3, third)):
         rotated = put(rotated, piece, shift)
     return (gram, rotated)

time: 104 us -> 103 us (level)
  waiting for transfers between devices: 29.6 us -> 25.4 us
  starting transfers between devices: 32.5 us -> 35.1 us
    ppermute x7 -> x6, waiting for transfers between devices: 7.61 us -> 2.23 us  [reduce_over(): total = total + lax.ppermute(sent, axis, pairs).astype(value.dtype)]
    ppermute x1 -> x3, starting transfers between devices: 2.47 us -> 6.13 us  [on_device(): lax.ppermute(sent, ('gx', 'gyz'), [(i, i ^ flip) for i in range(64)])]
    ppermute x1 -> x3, waiting for transfers between devices: 0.78 us -> 2 us  [on_device(): lax.ppermute(sent, ('gx', 'gyz'), [(i, i ^ flip) for i in range(64)])]
    ppermute x7 -> x6, starting transfers between devices: 5.28 us -> 4.84 us  [reduce_over(): total = total + lax.ppermute(sent, axis, pairs).astype(value.dtype)]
  transfers between devices with their start and end apart: 16 -> 17, of which waited for: 6 -> 5; matrix products, arithmetic and copies ran while one was open for 3% -> 3% of each run, Pallas kernels for 0% -> 0%
where the time goes in v5:
time: 103 us
  starting transfers between devices  35.1 us (34%)
  blocking collectives  25.5 us (25%)
  waiting for transfers between devices  25.4 us (25%)
  Pallas kernels  6.51 us (6%)
  matrix products  4.23 us (4%)
  local copies, waits for them, and re-layouts  2.75 us (3%)
  other arithmetic  2.13 us (2%)
  between operations  1.11 us (1%)
    all_to_all x1, blocking collectives, on_device(): taken = lax.all_to_all(message, ('gx', 'gyz'), 0, 0, tiled=True)  25.5 us
    all_to_all x1, waiting for transfers between devices, on_device(): lax.all_to_all(filtered.reshape(256, 8, 128), ('band', 'gx', 'gyz'), 0, 0...  20.7 us
    ppermute x6, starting transfers between devices, to_band(): return lax.ppermute(value, 'band', [(i, (i + shift) % 4) for i in range(4)])  14.5 us
    all_to_all x1, starting transfers between devices, on_device(): lax.all_to_all(filtered.reshape(256, 8, 128), ('band', 'gx', 'gyz'), 0, 0...  9.4 us
    pallas_call x1, Pallas kernels, run_filter(): pl.pallas_call(filter_kernel, out_shape=jax.ShapeDtypeStruct((4, 8, NY, N...  6.51 us
    ppermute x3, starting transfers between devices, on_device(): lax.ppermute(sent, ('gx', 'gyz'), [(i, i ^ flip) for i in range(64)])  6.13 us
    ppermute x6, starting transfers between devices, reduce_over(): total = total + lax.ppermute(sent, axis, pairs).astype(value.dtype)  4.84 us
    ppermute x6, waiting for transfers between devices, reduce_over(): total = total + lax.ppermute(sent, axis, pairs).astype(value.dtype)  2.23 us
  transfers between devices with their start and end apart: 17, of which 5 were waited for; matrix products, arithmetic and copies ran while one was open for 3% of the time, Pallas kernels for 0%

profile of v5, /device:TPU:1, one launch (start us, length us, event | category | flops | bytes accessed | tf_op | source)
XLA Modules:
  0.0 102.8 jit_solution(462961680435459986)
XLA Ops:
  0.6 0.9 pad.4
  1.7 1.8 %fusion.1 = bf16[256,4096]{1,0:T(8,128)(2,1)S(1)} fusion(bf16[256,11]{0,1:T(8,128)(2,1)} %param.12, bf16[11,4096]{1,0:T(8,128)(2,1)S(1)} %bitcast.80), kind=kOutput, calls=%fused_computation.5 | convolution fusion | flops 27262976 | bytes 2192896 | tf_op jit(solution)/shard_map/dot_general | solution.py:37
  3.5 1.4 %convolution_bitcast_fusion = f32[8,4096]{1,0:T(8,128)S(1)} fusion(bf16[256,4096]{1,0:T(8,128)(2,1)S(1)} %fusion.1, bf16[1,256,256]{2,1,0:T(8,128)(2,1)S(1)} %copy-done, bf16[256]{0:T(256)(128)(2,1)S(1)} %copy-done.6), kind=kOutput, calls=%fused_computation.7 | convolution fusion | flops 557842432 | bytes 2359808 | tf_op jit(solution)/shard_map/dot_general | solution.py:40
  5.4 25.5 %all_to_all.10 = f16[64,6,8,128]{3,2,1,0:T(8,128)(2,1)S(1)} all-to-all(f16[64,6,8,128]{3,2,1,0:T(8,128)(2,1)S(1)} %pad_maximum_fusion), channel_id=1, replica_groups=mesh['gx'=8,'gyz'=8,'band'=4] {'gx','gyz'}, dimensions={0} | all-to-all | bytes 1572864 | tf_op jit(solution)/shard_map/all_to_all | solution.py:181
  30.9 0.3 collective-permute-start
  31.2 0.6 dynamic_slice.30
  31.8 0.7 pad_add_fusion.info
  32.7 6.5 %shard_map.104 = bf16[4,8,64,128]{3,2,1,0:T(8,128)(2,1)} custom-call(s32[2]{0:T(128)S(1)} %pad_add_fusion.info, f32[64,6,8,128]{3,2,1,0:T(8,128)S(1)} %convert_element_type.107.taken, f32[64,2,8,128]{3,2,1,0:T(8,128)S(1)} %convert_element_type.108.other), custom_call_target="tpu_custom_call" | custom-call | flops 33554432 | bytes 3145728 | tf_op jit(solution)/shard_map/pallas_call | solution.py:130
  39.2 9.4 %all-to-all-start.1 = ((bf16[256,8,128]{2,1,0:T(8,128)(2,1)}), bf16[256,8,128]{2,1,0:T(8,128)(2,1)S(1)}, u32[]{:S(2)}, u32[]{:S(2)}) async-start(bf16[256,8,128]{2,1,0:T(8,128)(2,1)} %bitcast.7), calls=%async_computation.1 | async-start | bytes 1048576 | tf_op jit(solution)/shard_map/all_to_all | solution.py:193
  48.7 0.4 convolution_convert_fusion.1
  49.1 20.7 %all-to-all-done.1 = bf16[256,8,128]{2,1,0:T(8,128)(2,1)S(1)} async-done(((bf16[256,8,128]{2,1,0:T(8,128)(2,1)}), bf16[256,8,128]{2,1,0:T(8,128)(2,1)S(1)}, u32[]{:S(2)}, u32[]{:S(2)}) %all-to-all-start.1) | async-done | bytes 524320 | tf_op jit(solution)/shard_map/all_to_all | solution.py:193
  69.7 0.3 copy.17
  70.0 0.3 fusion.3
  70.4 0.9 collective-permute-start.3
  71.3 2.9 %collective-permute-start.2 = (bf16[64,256]{1,0:T(8,128)(2,1)S(1)}, bf16[64,256]{1,0:T(8,128)(2,1)S(1)}, u32[]{:S(2)}, u32[]{:S(2)}) collective-permute-start(bf16[64,256]{1,0:T(8,128)(2,1)S(1)} %get-tuple-element.30), channel_id=1, source_target_pairs={{0,2},{1,3},{2,0},{3,1},{4,6},{5,7},{6,4},{7,5},{8,10},{9,11},{10,... | collective-permute-start | bytes 98312 | tf_op jit(solution)/shard_map/ppermute | solution.py:160
  74.2 0.3 convolution_convert_fusion
  74.7 4.3 %collective-permute-start.7 = (bf16[64,1024]{1,0:T(8,128)(2,1)S(1)}, bf16[64,1024]{1,0:T(8,128)(2,1)S(1)}, u32[]{:S(2)}, u32[]{:S(2)}) collective-permute-start(bf16[64,1024]{1,0:T(8,128)(2,1)S(1)} %get-tuple-element.26), channel_id=1, source_target_pairs={{0,2},{1,3},{2,0},{3,1},{4,6},{5,7},{6,4},{7,5},{8,10},{9,11},{10,... | collective-permute-start | bytes 393224 | tf_op jit(solution)/shard_map/ppermute | solution.py:160
  79.0 0.6 collective-permute-done.1
  79.6 1.1 %collective-permute-start.6 = (bf16[64,256]{1,0:T(8,128)(2,1)S(1)}, bf16[64,256]{1,0:T(8,128)(2,1)S(1)}, u32[]{:S(2)}, u32[]{:S(2)}) collective-permute-start(bf16[64,256]{1,0:T(8,128)(2,1)S(1)} %convert_element_type.122), channel_id=1, source_target_pairs={{0,192},{32,224},{64,0},{96,32},{128,64},{160,96},{192,128},{224,1... | collective-permute-start | bytes 98312 | tf_op jit(solution)/shard_map/ppermute | solution.py:155
  80.7 0.8 collective-permute-start.5
  81.5 0.5 collective-permute-start.4
  82.1 1.3 %collective-permute-start.11 = (bf16[64,1024]{1,0:T(8,128)(2,1)S(1)}, bf16[64,1024]{1,0:T(8,128)(2,1)S(1)}, u32[]{:S(2)}, u32[]{:S(2)}) collective-permute-start(bf16[64,1024]{1,0:T(8,128)(2,1)S(1)} %get-tuple-element.17), channel_id=1, source_target_pairs={{0,1},{1,2},{2,3},{3,0},{4,5},{5,6},{6,7},{7,4},{8,9},{9,10},{10,1... | collective-permute-start | bytes 393224 | tf_op jit(solution)/shard_map/ppermute | solution.py:160
  83.4 1.9 %collective-permute-done.5 = bf16[64,256]{1,0:T(8,128)(2,1)S(1)} collective-permute-done((bf16[64,256]{1,0:T(8,128)(2,1)S(1)}, bf16[64,256]{1,0:T(8,128)(2,1)S(1)}, u32[]{:S(2)}, u32[]{:S(2)}) %collective-permute-start.5) | collective-permute-done | bytes 32800 | tf_op jit(solution)/shard_map/ppermute | solution.py:155
  85.3 0.3 collective-permute-done.4
  85.6 1.6 %collective-permute-start.10 = (bf16[64,256]{1,0:T(8,128)(2,1)S(1)}, bf16[64,256]{1,0:T(8,128)(2,1)S(1)}, u32[]{:S(2)}, u32[]{:S(2)}) collective-permute-start(bf16[64,256]{1,0:T(8,128)(2,1)S(1)} %convert_element_type.126), channel_id=1, source_target_pairs={{0,24},{4,28},{8,0},{12,4},{16,8},{20,12},{24,16},{28,20},{1,25},{... | collective-permute-start | bytes 98312 | tf_op jit(solution)/shard_map/ppermute | solution.py:155
  87.3 0.7 collective-permute-start.9
  88.1 5.1 %collective-permute-start.13 = (bf16[64,1024]{1,0:T(8,128)(2,1)S(1)}, bf16[64,1024]{1,0:T(8,128)(2,1)S(1)}, u32[]{:S(2)}, u32[]{:S(2)}) collective-permute-start(bf16[64,1024]{1,0:T(8,128)(2,1)S(1)} %get-tuple-element.19), channel_id=1, source_target_pairs={{0,3},{1,0},{2,1},{3,2},{4,7},{5,4},{6,5},{7,6},{8,11},{9,8},{10,9... | collective-permute-start | bytes 393224 | tf_op jit(solution)/shard_map/ppermute | solution.py:160
  93.4 4.4 %collective-permute-start.15 = (bf16[64,256]{1,0:T(8,128)(2,1)S(1)}, bf16[64,256]{1,0:T(8,128)(2,1)S(1)}, u32[]{:S(2)}, u32[]{:S(2)}) collective-permute-start(bf16[64,256]{1,0:T(8,128)(2,1)S(1)} %convert_element_type.130), channel_id=1, source_target_pairs={{0,32},{4,36},{8,40},{12,44},{16,48},{20,52},{24,56},{28,60},{32,0... | collective-permute-start | bytes 98312 | tf_op jit(solution)/shard_map/ppermute | solution.py:231
  97.8 1.7 %collective-permute-start.12 = (bf16[64,256]{1,0:T(8,128)(2,1)S(1)}, bf16[64,256]{1,0:T(8,128)(2,1)S(1)}, u32[]{:S(2)}, u32[]{:S(2)}) collective-permute-start(bf16[64,256]{1,0:T(8,128)(2,1)S(1)} %convert_element_type.130), channel_id=1, source_target_pairs={{0,36},{4,32},{8,44},{12,40},{16,52},{20,48},{24,60},{28,56},{32,4... | collective-permute-start | bytes 98312 | tf_op jit(solution)/shard_map/ppermute | solution.py:231
  99.7 2.0 %collective-permute-done.12 = bf16[64,256]{1,0:T(8,128)(2,1)S(1)} collective-permute-done((bf16[64,256]{1,0:T(8,128)(2,1)S(1)}, bf16[64,256]{1,0:T(8,128)(2,1)S(1)}, u32[]{:S(2)}, u32[]{:S(2)}) %collective-permute-start.12) | collective-permute-done | bytes 32800 | tf_op jit(solution)/shard_map/ppermute | solution.py:231
  101.8 0.7 add_add_fusion
  102.5 0.2 copy-done.2
  (59 shorter events, 1.5 us)
Async XLA Ops:
  0.6 2.8 %copy-start = (bf16[1,256,256]{2,1,0:T(8,128)(2,1)S(1)}, bf16[1,256,256]{2,1,0:T(8,128)(2,1)}, u32[]{:S(2)}) copy-start(bf16[1,256,256]{2,1,0:T(8,128)(2,1)} %param.13) | copy-start | bytes 393220
  1.6 1.8 %copy-start.6 = (bf16[256]{0:T(256)(128)(2,1)S(1)}, bf16[256]{0:T(256)(128)(2,1)}, u32[]{:S(2)}) copy-start(bf16[256]{0:T(256)(128)(2,1)} %param.14) | copy-start | bytes 1540
  3.5 1.5 %copy-start.1 = (f32[64,4,8,128]{3,2,1,0:T(8,128)S(1)}, f32[64,4,8,128]{3,2,1,0:T(8,128)}, u32[]{:S(2)}) copy-start(f32[64,4,8,128]{3,2,1,0:T(8,128)} %param.9) | copy-start | bytes 3145732
  3.5 1.6 %copy-start.4 = (f32[4,8,128]{2,1,0:T(8,128)S(1)}, f32[4,8,128]{2,1,0:T(8,128)}, u32[]{:S(2)}) copy-start(f32[4,8,128]{2,1,0:T(8,128)} %param.10) | copy-start | bytes 49156
  5.1 26.1 %copy-start.7 = (s32[64]{0:T(128)S(1)}, s32[64]{0:T(128)}, u32[]{:S(2)}) copy-start(s32[64]{0:T(128)} %param.17) | copy-start | bytes 772
  30.9 1.8 %collective-permute-start = (f16[64,2,8,128]{3,2,1,0:T(8,128)(2,1)S(1)}, f16[64,2,8,128]{3,2,1,0:T(8,128)(2,1)S(1)}, u32[]{:S(2)}, u32[]{:S(2)}) collective-permute-start(f16[64,2,8,128]{3,2,1,0:T(8,128)(2,1)S(1)} %slice.9), channel_id=1, source_target_pairs={{0,32},{32,0},{64,96},{96,64},{128,160},{160,128},{192,224},{224,1... | collective-permute-start | bytes 786440 | tf_op jit(solution)/shard_map/ppermute | solution.py:182
  32.6 16.0 %copy-start.3 = (f32[256,256]{1,0:T(8,128)S(1)}, f32[256,256]{1,0:T(8,128)}, u32[]{:S(2)}) copy-start(f32[256,256]{1,0:T(8,128)} %param.15) | copy-start | bytes 786436
  32.6 16.0 %copy-start.5 = (s32[256]{0:T(256)S(1)}, s32[256]{0:T(256)}, u32[]{:S(2)}) copy-start(s32[256]{0:T(256)} %param.16) | copy-start | bytes 3076
  39.2 30.5 %all-to-all-start.1 = ((bf16[256,8,128]{2,1,0:T(8,128)(2,1)}), bf16[256,8,128]{2,1,0:T(8,128)(2,1)S(1)}, u32[]{:S(2)}, u32[]{:S(2)}) async-start(bf16[256,8,128]{2,1,0:T(8,128)(2,1)} %bitcast.7), calls=%async_computation.1 | async-start | bytes 1048576 | tf_op jit(solution)/shard_map/all_to_all | solution.py:193
  70.4 8.6 %collective-permute-start.3 = (bf16[64,256]{1,0:T(8,128)(2,1)S(1)}, bf16[64,256]{1,0:T(8,128)(2,1)S(1)}, u32[]{:S(2)}, u32[]{:S(2)}) collective-permute-start(bf16[64,256]{1,0:T(8,128)(2,1)S(1)} %get-tuple-element.29), channel_id=1, source_target_pairs={{0,3},{1,0},{2,1},{3,2},{4,7},{5,4},{6,5},{7,6},{8,11},{9,8},{10,9... | collective-permute-start | bytes 98312 | tf_op jit(solution)/shard_map/ppermute | solution.py:160
  71.3 7.7 %collective-permute-start.2 = (bf16[64,256]{1,0:T(8,128)(2,1)S(1)}, bf16[64,256]{1,0:T(8,128)(2,1)S(1)}, u32[]{:S(2)}, u32[]{:S(2)}) collective-permute-start(bf16[64,256]{1,0:T(8,128)(2,1)S(1)} %get-tuple-element.30), channel_id=1, source_target_pairs={{0,2},{1,3},{2,0},{3,1},{4,6},{5,7},{6,4},{7,5},{8,10},{9,11},{10,... | collective-permute-start | bytes 98312 | tf_op jit(solution)/shard_map/ppermute | solution.py:160
  74.2 5.3 %collective-permute-start.1 = (bf16[64,256]{1,0:T(8,128)(2,1)S(1)}, bf16[64,256]{1,0:T(8,128)(2,1)S(1)}, u32[]{:S(2)}, u32[]{:S(2)}) collective-permute-start(bf16[64,256]{1,0:T(8,128)(2,1)S(1)} %get-tuple-element.28), channel_id=1, source_target_pairs={{0,1},{1,2},{2,3},{3,0},{4,5},{5,6},{6,7},{7,4},{8,9},{9,10},{10,1... | collective-permute-start | bytes 98312 | tf_op jit(solution)/shard_map/ppermute | solution.py:160
  74.7 11.0 %collective-permute-start.7 = (bf16[64,1024]{1,0:T(8,128)(2,1)S(1)}, bf16[64,1024]{1,0:T(8,128)(2,1)S(1)}, u32[]{:S(2)}, u32[]{:S(2)}) collective-permute-start(bf16[64,1024]{1,0:T(8,128)(2,1)S(1)} %get-tuple-element.26), channel_id=1, source_target_pairs={{0,2},{1,3},{2,0},{3,1},{4,6},{5,7},{6,4},{7,5},{8,10},{9,11},{10,... | collective-permute-start | bytes 393224 | tf_op jit(solution)/shard_map/ppermute | solution.py:160
  79.6 3.8 %collective-permute-start.6 = (bf16[64,256]{1,0:T(8,128)(2,1)S(1)}, bf16[64,256]{1,0:T(8,128)(2,1)S(1)}, u32[]{:S(2)}, u32[]{:S(2)}) collective-permute-start(bf16[64,256]{1,0:T(8,128)(2,1)S(1)} %convert_element_type.122), channel_id=1, source_target_pairs={{0,192},{32,224},{64,0},{96,32},{128,64},{160,96},{192,128},{224,1... | collective-permute-start | bytes 98312 | tf_op jit(solution)/shard_map/ppermute | solution.py:155
  80.7 4.6 %collective-permute-start.5 = (bf16[64,256]{1,0:T(8,128)(2,1)S(1)}, bf16[64,256]{1,0:T(8,128)(2,1)S(1)}, u32[]{:S(2)}, u32[]{:S(2)}) collective-permute-start(bf16[64,256]{1,0:T(8,128)(2,1)S(1)} %convert_element_type.122), channel_id=1, source_target_pairs={{0,128},{32,160},{64,192},{96,224},{128,0},{160,32},{192,64},{224,... | collective-permute-start | bytes 98312 | tf_op jit(solution)/shard_map/ppermute | solution.py:155
  81.5 4.1 %collective-permute-start.4 = (bf16[64,256]{1,0:T(8,128)(2,1)S(1)}, bf16[64,256]{1,0:T(8,128)(2,1)S(1)}, u32[]{:S(2)}, u32[]{:S(2)}) collective-permute-start(bf16[64,256]{1,0:T(8,128)(2,1)S(1)} %convert_element_type.122), channel_id=1, source_target_pairs={{0,64},{32,96},{64,128},{96,160},{128,192},{160,224},{192,0},{224,... | collective-permute-start | bytes 98312 | tf_op jit(solution)/shard_map/ppermute | solution.py:155
  82.1 11.3 %collective-permute-start.11 = (bf16[64,1024]{1,0:T(8,128)(2,1)S(1)}, bf16[64,1024]{1,0:T(8,128)(2,1)S(1)}, u32[]{:S(2)}, u32[]{:S(2)}) collective-permute-start(bf16[64,1024]{1,0:T(8,128)(2,1)S(1)} %get-tuple-element.17), channel_id=1, source_target_pairs={{0,1},{1,2},{2,3},{3,0},{4,5},{5,6},{6,7},{7,4},{8,9},{9,10},{10,1... | collective-permute-start | bytes 393224 | tf_op jit(solution)/shard_map/ppermute | solution.py:160
  85.6 7.7 %collective-permute-start.10 = (bf16[64,256]{1,0:T(8,128)(2,1)S(1)}, bf16[64,256]{1,0:T(8,128)(2,1)S(1)}, u32[]{:S(2)}, u32[]{:S(2)}) collective-permute-start(bf16[64,256]{1,0:T(8,128)(2,1)S(1)} %convert_element_type.126), channel_id=1, source_target_pairs={{0,24},{4,28},{8,0},{12,4},{16,8},{20,12},{24,16},{28,20},{1,25},{... | collective-permute-start | bytes 98312 | tf_op jit(solution)/shard_map/ppermute | solution.py:155
  87.3 6.1 %collective-permute-start.9 = (bf16[64,256]{1,0:T(8,128)(2,1)S(1)}, bf16[64,256]{1,0:T(8,128)(2,1)S(1)}, u32[]{:S(2)}, u32[]{:S(2)}) collective-permute-start(bf16[64,256]{1,0:T(8,128)(2,1)S(1)} %convert_element_type.126), channel_id=1, source_target_pairs={{0,16},{4,20},{8,24},{12,28},{16,0},{20,4},{24,8},{28,12},{1,17},{... | collective-permute-start | bytes 98312 | tf_op jit(solution)/shard_map/ppermute | solution.py:155
  88.0 5.4 %collective-permute-start.8 = (bf16[64,256]{1,0:T(8,128)(2,1)S(1)}, bf16[64,256]{1,0:T(8,128)(2,1)S(1)}, u32[]{:S(2)}, u32[]{:S(2)}) collective-permute-start(bf16[64,256]{1,0:T(8,128)(2,1)S(1)} %convert_element_type.126), channel_id=1, source_target_pairs={{0,8},{4,12},{8,16},{12,20},{16,24},{20,28},{24,0},{28,4},{1,9},{5... | collective-permute-start | bytes 98312 | tf_op jit(solution)/shard_map/ppermute | solution.py:155
  88.1 13.5 %collective-permute-start.13 = (bf16[64,1024]{1,0:T(8,128)(2,1)S(1)}, bf16[64,1024]{1,0:T(8,128)(2,1)S(1)}, u32[]{:S(2)}, u32[]{:S(2)}) collective-permute-start(bf16[64,1024]{1,0:T(8,128)(2,1)S(1)} %get-tuple-element.19), channel_id=1, source_target_pairs={{0,3},{1,0},{2,1},{3,2},{4,7},{5,4},{6,5},{7,6},{8,11},{9,8},{10,9... | collective-permute-start | bytes 393224 | tf_op jit(solution)/shard_map/ppermute | solution.py:160
  93.4 8.4 %collective-permute-start.15 = (bf16[64,256]{1,0:T(8,128)(2,1)S(1)}, bf16[64,256]{1,0:T(8,128)(2,1)S(1)}, u32[]{:S(2)}, u32[]{:S(2)}) collective-permute-start(bf16[64,256]{1,0:T(8,128)(2,1)S(1)} %convert_element_type.130), channel_id=1, source_target_pairs={{0,32},{4,36},{8,40},{12,44},{16,48},{20,52},{24,56},{28,60},{32,0... | collective-permute-start | bytes 98312 | tf_op jit(solution)/shard_map/ppermute | solution.py:231
  97.8 4.0 %collective-permute-start.14 = (bf16[64,256]{1,0:T(8,128)(2,1)S(1)}, bf16[64,256]{1,0:T(8,128)(2,1)S(1)}, u32[]{:S(2)}, u32[]{:S(2)}) collective-permute-start(bf16[64,256]{1,0:T(8,128)(2,1)S(1)} %convert_element_type.130), channel_id=1, source_target_pairs={{0,4},{4,0},{8,12},{12,8},{16,20},{20,16},{24,28},{28,24},{32,36},... | collective-permute-start | bytes 98312 | tf_op jit(solution)/shard_map/ppermute | solution.py:231
  97.8 3.8 %collective-permute-start.12 = (bf16[64,256]{1,0:T(8,128)(2,1)S(1)}, bf16[64,256]{1,0:T(8,128)(2,1)S(1)}, u32[]{:S(2)}, u32[]{:S(2)}) collective-permute-start(bf16[64,256]{1,0:T(8,128)(2,1)S(1)} %convert_element_type.130), channel_id=1, source_target_pairs={{0,36},{4,32},{8,44},{12,40},{16,52},{20,48},{24,60},{28,56},{32,4... | collective-permute-start | bytes 98312 | tf_op jit(solution)/shard_map/ppermute | solution.py:231
  101.8 1.0 copy-start.2
